TPU v7x, 32 devices: a whole 2x2x4 slice. The times are simulated.
32 devices in a mesh: grp: 8 (over y, x, core), tp: 4 (over z).
Axes of the slice: x: 2, y: 2, z: 4, core: 2. Of those that a mesh axis runs over, the one named last changes fastest.
Arguments:
- x_rows: bfloat16 [8192, 4096], P(('grp', 'tp')), may hold values from -6 to 6
- norm_gain: float32 [4096], replicated, may hold values from 0.1 to 1.9
- w_query: bfloat16 [4096, 4096], P(None, 'tp'), may hold values from -0.25 to 0.25
- w_keyval: bfloat16 [4096, 2, 1024], P(None, None, 'tp'), may hold values from -0.09375 to 0.09375
- w_out: bfloat16 [4096, 4096], P('tp'), may hold values from -0.75 to 0.75
- prefix_cache: bfloat16 [16, 128, 2, 1024], P('grp', None, None, 'tp'), may hold values from -70 to 70, as said below
- page_table: int32 [16], replicated, may hold values from 0 to 15, each once
- request_ids: int32 [8192], replicated, may hold values from 0 to 15, never falling along the last dimension, each value on 1 to 1024 neighbouring positions
Outputs:
- attn_out: bfloat16 [8192, 4096], P(('grp', 'tp'))
Inputs may be any that keep to these rules, and one draw needn't show every extreme that they name: `request_ids`: request ids never fall along the stream; each of the 16 requests has 1 to 1024 tokens, one exactly 1024. `page_table`: a permutation; physical page f belongs to group f // 2. `prefix_cache`: keys are stored already rotated for their positions.
All inputs are finite; a program needn't handle non-finite values.
Results may differ from a plain program's by a relative error of at most 0.025.
The roundings to bfloat16 on the way count: a program that leaves them out, or rounds other values in their place, can miss the bound.
Values may be sent and summed in bfloat16 or wider, within the bound.
No kernel may reach another device: no remote copies, remote signals or barrier semaphores. Data moves between devices by JAX's collectives and lax.ppermute only.
A program may use at most 128 MiB of HBM per device.

v0:
```python
import jax
import jax.numpy as jnp
from jax import lax
from jax.sharding import PartitionSpec as P

KVH = 8
HD = 128
SINKS = 4


def shortened(array):

    def short(part):
        return part.astype(jnp.bfloat16) if part.dtype == jnp.float32 else part

    return jax.tree.map(short, array)


def swapped(block, axis, apart):
    count = lax.axis_size(axis)
    route = []
    for low in range(count):
        high = low | 1 << apart
        if high != low and high < count:
            route += [(low, high), (high, low)]
    return lax.ppermute(block, axis, route)


def shifted(block, axis, distance):
    devices = range(lax.axis_size(axis))
    route = [(i - distance, i) for i in devices if i - distance in devices]
    return lax.ppermute(block, axis, route)


def rotate(values, positions):
    half = HD // 2
    freqs = 500000.0 ** (-jnp.arange(half, dtype=jnp.float32) * 2.0 / HD)
    angles = positions.astype(jnp.float32)[:, None] * freqs[None, :]
    cosine = jnp.cos(angles)[:, None, :]
    sine = jnp.sin(angles)[:, None, :]
    first = values[..., :half]
    second = values[..., half:]
    return jnp.concatenate(
        [first * cosine - second * sine, second * cosine + first * sine], axis=-1
    )


def segment_first(request_ids, wanted, count):
    labels = jnp.arange(count, dtype=jnp.int32)
    counts = jnp.sum((request_ids[:, None] == labels[None, :]).astype(jnp.int32), axis=0)
    starts = jnp.cumsum(counts) - counts
    match = wanted[:, None] == labels[None, :]
    return jnp.sum(jnp.where(match, starts[None, :], 0), axis=1)


def join_pair(lower, mine, peer):
    return jnp.where(
        lower, jnp.concatenate([mine, peer], axis=2), jnp.concatenate([peer, mine], axis=2)
    )


def fold_block(state, queries, keys, values, visible):
    run_max, run_sum, run_acc = state
    scores = jnp.einsum(
        "qgrd,kgd->qgrk", queries, keys, preferred_element_type=jnp.float32
    ) * HD ** (-0.5)
    allowed = visible[:, None, None, :]
    scores = jnp.where(allowed, scores, -1e30)
    new_max = jnp.maximum(run_max, jnp.max(scores, axis=-1))
    weights = jnp.where(allowed, jnp.exp(scores - new_max[..., None]), 0.0)
    factor = jnp.exp(run_max - new_max)
    new_sum = run_sum * factor + jnp.sum(weights, axis=-1)
    new_acc = run_acc * factor[..., None] + jnp.einsum(
        "qgrk,kgd->qgrd", weights.astype(jnp.bfloat16), values, preferred_element_type=jnp.float32
    )
    return (new_max, new_sum, new_acc)


def fold_all(
    state, queries, query_pos, query_seg, query_index, keys, values, visible_fn, block_rows
):
    blocks = queries.shape[0] // block_rows

    def in_blocks(array):
        return array.reshape((blocks, block_rows) + array.shape[1:])

    def update_block(item):
        part_state, part_queries, part_pos, part_seg, part_index = item
        return fold_block(
            part_state, part_queries, keys, values, visible_fn(part_pos, part_seg, part_index)
        )

    pieces = (
        tuple((in_blocks(member) for member in state)),
        in_blocks(queries),
        in_blocks(query_pos),
        in_blocks(query_seg),
        in_blocks(query_index),
    )
    result = lax.map(update_block, pieces)
    return tuple((member.reshape((-1,) + member.shape[2:]) for member in result))


def local(x_rows, norm_gain, w_query, w_keyval, w_out, prefix_cache, page_table, request_ids):
    tp_size = lax.axis_size("tp")
    grp_size = lax.axis_size("grp")
    tp_index = lax.axis_index("tp")
    grp_index = lax.axis_index("grp")
    tok_dev = x_rows.shape[0]
    tok_group = tok_dev * tp_size
    heads_dev = w_query.shape[1] // HD
    kv_cols = w_keyval.shape[2]
    kv_need = max(HD, HD * KVH // tp_size)
    kv_heads = kv_need // HD
    per_kv = heads_dev // kv_heads
    pages_dev = prefix_cache.shape[0]
    page_len = prefix_cache.shape[1]
    prefix_len = pages_dev * grp_size * page_len
    seg_count = 2 * grp_size
    block_rows = min(512, tok_group)
    pair_bits = (kv_need // kv_cols).bit_length() - 1
    wide = x_rows.astype(jnp.float32)
    variance = jnp.mean(wide * wide, axis=-1, keepdims=True) + 1e-05
    inverse = lax.rsqrt(variance)
    normed = (wide * inverse * norm_gain).astype(jnp.bfloat16)
    kv_weight = w_keyval.reshape(w_keyval.shape[0], 2 * kv_cols)
    piece = lax.all_gather(normed, "tp", axis=0, tiled=True)
    query_part = jnp.dot(piece, w_query, preferred_element_type=jnp.float32)
    kv_part = jnp.dot(piece, kv_weight, preferred_element_type=jnp.float32)
    projected = jnp.concatenate([query_part, kv_part], axis=1)
    query_cols = heads_dev * HD
    group_start = grp_index * tok_group
    token_index = group_start + jnp.arange(tok_group, dtype=jnp.int32)
    own_seg = lax.dynamic_slice_in_dim(request_ids, group_start, tok_group, 0)
    own_pos = prefix_len + token_index - segment_first(request_ids, own_seg, seg_count)
    queries = rotate(projected[:, :query_cols].reshape(tok_group, heads_dev, HD), own_pos).astype(
        jnp.bfloat16
    )
    queries = queries.reshape(tok_group, kv_heads, per_kv, HD)
    kv_local = projected[:, query_cols:].astype(jnp.bfloat16).reshape(tok_group, 2, kv_cols)
    cache_local = prefix_cache.reshape(pages_dev * page_len, 2, kv_cols)
    kv_own = kv_local
    cache_own = cache_local
    for bit_num in range(pair_bits):
        kv_peer, cache_peer = (
            swapped(shortened(kv_own), "tp", bit_num).astype(kv_own.dtype),
            swapped(shortened(cache_own), "tp", bit_num).astype(cache_own.dtype),
        )
        lower = tp_index >> bit_num & 1 == 0
        kv_own = join_pair(lower, kv_own, kv_peer)
        cache_own = join_pair(lower, cache_own, cache_peer)
    keys_own = rotate(
        kv_own[:, 0].reshape(tok_group, kv_heads, HD).astype(jnp.float32), own_pos
    ).astype(jnp.bfloat16)
    values_own = kv_own[:, 1].reshape(tok_group, kv_heads, HD)
    keys_prev, values_prev = shifted((keys_own, values_own), "grp", 1)
    prev_start = jnp.maximum(group_start - tok_group, 0)
    prev_index = group_start - tok_group + jnp.arange(tok_group, dtype=jnp.int32)
    prev_seg = jnp.where(
        grp_index > 0, lax.dynamic_slice_in_dim(request_ids, prev_start, tok_group, 0), -1
    )
    prev_pos = prefix_len + prev_index - segment_first(request_ids, prev_seg, seg_count)
    suffix_keys = jnp.concatenate([keys_prev, keys_own], axis=0)
    suffix_values = jnp.concatenate([values_prev, values_own], axis=0)
    suffix_seg = jnp.concatenate([prev_seg, own_seg], axis=0)
    suffix_pos = jnp.concatenate([prev_pos, own_pos], axis=0)
    suffix_index = jnp.concatenate([prev_index, token_index], axis=0)

    def suffix_visible(query_pos, query_seg, query_index):
        same = (suffix_seg[None, :] == query_seg[:, None]) & (
            suffix_index[None, :] <= query_index[:, None]
        )
        return same & (
            (query_pos[:, None] - suffix_pos[None, :] < prefix_len) | (suffix_pos[None, :] < SINKS)
        )

    start_state = (
        jnp.full((tok_group, kv_heads, per_kv), -1e30, jnp.float32),
        jnp.zeros((tok_group, kv_heads, per_kv), jnp.float32),
        jnp.zeros((tok_group, kv_heads, per_kv, HD), jnp.float32),
    )
    state = fold_all(
        start_state,
        queries,
        own_pos,
        own_seg,
        token_index,
        suffix_keys,
        suffix_values,
        suffix_visible,
        block_rows,
    )
    page_labels = jnp.arange(page_table.shape[0], dtype=jnp.int32)
    cache_keys = cache_own[:, 0].reshape(pages_dev * page_len, kv_heads, HD)
    cache_values = cache_own[:, 1].reshape(pages_dev * page_len, kv_heads, HD)
    piece_keys = lax.all_gather(cache_keys, "grp", axis=0, tiled=True)
    piece_values = lax.all_gather(cache_values, "grp", axis=0, tiled=True)
    rows = piece_keys.shape[0]
    physical = jnp.arange(rows // page_len, dtype=jnp.int32)
    logical = jnp.sum(
        jnp.where(page_table[None, :] == physical[:, None], page_labels[None, :], 0), axis=1
    )
    key_pos = (
        logical[:, None] * page_len + jnp.arange(page_len, dtype=jnp.int32)[None, :]
    ).reshape(rows)

    def prefix_visible(query_pos, query_seg, query_index):
        before = key_pos[None, :] <= query_pos[:, None]
        return before & (
            (query_pos[:, None] - key_pos[None, :] < prefix_len) | (key_pos[None, :] < SINKS)
        )

    state = fold_all(
        state,
        queries,
        own_pos,
        own_seg,
        token_index,
        piece_keys,
        piece_values,
        prefix_visible,
        block_rows,
    )
    attn = (state[2] / state[1][..., None]).reshape(tok_group, heads_dev * HD).astype(jnp.bfloat16)
    rows = attn
    return lax.psum_scatter(
        jnp.dot(rows, w_out, preferred_element_type=jnp.float32).astype(jnp.bfloat16),
        "tp",
        scatter_dimension=0,
        tiled=True,
    )


def solution(mesh):
    placed = (
        P(("grp", "tp"), None),
        P(),
        P(None, "tp"),
        P(None, None, "tp"),
        P("tp", None),
        P("grp", None, None, "tp"),
        P(),
        P(),
    )
    return jax.shard_map(
        local, mesh=mesh, in_specs=placed, out_specs=P(("grp", "tp"), None), check_vma=False
    )
```

profile of v0, /device:TPU:2, one launch (start us, length us, event | category | flops | bytes accessed | tf_op | source)
XLA Modules:
  0.0 637.4 jit_solution(9368573885146363334)
XLA Ops:
  14.8 4.9 copy.46
  21.5 12.6 %all-gather.6.cloned.1.call-done = bf16[2048,2,128]{0,2,1:T(8,128)(2,1)} async-done(((bf16[256,2,128]{0,2,1:T(8,128)(2,1)}), bf16[2048,2,128]{0,2,1:T(8,128)(2,1)}) %all-gather.6.cloned.1.call-update) | async-done | bytes 1048592 | tf_op jit(solution)/shard_map/all_gather | solution.py:196
  34.1 2.3 copy.29
  36.3 23.2 %all-gather.8.cloned.1.call-done = bf16[2048,2,128]{0,2,1:T(8,128)(2,1)} async-done(((bf16[256,2,128]{0,2,1:T(8,128)(2,1)}), bf16[2048,2,128]{0,2,1:T(8,128)(2,1)}) %all-gather.8.cloned.1.call-update) | async-done | bytes 1048592 | tf_op jit(solution)/shard_map/all_gather | solution.py:197
  59.6 2.3 copy.30
  61.8 149.0 %all-gather.4.cloned.1.call-done = bf16[1024,4096]{1,0:T(8,128)(2,1)} async-done(((bf16[256,4096]{1,0:T(8,128)(2,1)}), bf16[1024,4096]{1,0:T(8,128)(2,1)}) %all-gather.4.cloned.1.call-update) | async-done | bytes 8388624 | tf_op jit(solution)/shard_map/all_gather | solution.py:127
  210.8 9.1 %convolution_convert_fusion.1 = bf16[1024,512]{0,1:T(8,128)(2,1)S(1)} fusion(bf16[1024,4096]{1,0:T(8,128)(2,1)} %all-gather.4.cloned.1.call-done, bf16[4096,512]{1,0:T(8,128)(2,1)} %bitcast.188), kind=kOutput, calls=%fused_computation.84 | convolution fusion | flops 4295491584 | bytes 13631488 | tf_op jit(solution)/shard_map/dot_general | solution.py:129
  224.2 13.2 %fusion.59 = f32[1024,1024]{0,1:T(8,128)S(1)} fusion(bf16[1024,4096]{1,0:T(8,128)(2,1)} %all-gather.4.cloned.1.call-done, bf16[4096,1024]{1,0:T(8,128)(2,1)} %param.14), kind=kOutput, calls=%fused_computation.116 | convolution fusion | flops 8589934592 | bytes 20971520 | tf_op jit(solution)/shard_map/dot_general | solution.py:128
  240.5 3.4 collective-permute-start.1
  244.0 3.9 pad_maximum_fusion
  247.9 4.2 copy.24
  256.5 98.4 %while.27 = (s32[]{:T(128)}, f32[2,512,2,4]{1,3,2,0:T(4,128)S(1)}, f32[2,512,2,4]{1,3,2,0:T(4,128)S(1)}, f32[2,512,2,4,128]{4,1,3,2,0:T(8,128)}, s32[2048]{0:T(1...) while((s32[]{:T(128)}, f32[2,512,2,4]{1,3,2,0:T(4,128)S(1)}, ...), condition=%wide.region_8.9_spmd, body=%wide.region_5.8_spmd.sunk | while | flops 4411906048 | bytes 111401112 | solution.py:100
  258.7 15.3 %bitcast_reduce_fusion.4 = (f32[512,2,4]{0,2,1:T(4,128)S(1)}, f32[2,512,4,2048]{3,1,2,0:T(8,128)}) fusion(pred[512,2048]{1,0:T(8,128)(4,1)S(1)} %fusion.79, bf16[2048,2,128]{2,0,1:T(8,128)(2,1)} %get-tuple-element.497, bf16[2,512,2,4,128]{4,1,3,2,0:T(8,128)(2,1)} %get-tuple-element.496, s32[]{:T(128)S(6)} %copy.59), kind=kOutput, calls=%fused_computation.2.clone.1 | convolution fusion | flops 2172645376 | bytes 36716548 | tf_op jit(solution)/shard_map/while/body/eval_jaxpr/qgrd,kgd->qgrk/dot_general | solution.py:64
  274.0 15.6 %fusion.80 = f32[512,2,4]{0,2,1:T(4,128)S(1)} fusion(f32[2,512,4,2048]{3,1,2,0:T(8,128)} %get-tuple-element.437, f32[512,2,4]{0,2,1:T(4,128)S(1)} %get-tuple-element.439, pred[512,2048]{1,0:T(8,128)(4,1)S(1)} %fusion.79), kind=kLoop, calls=%fused_computation.7.clone.1 | loop fusion | flops 41938944 | bytes 34635776 | tf_op jit(solution)/shard_map/while/body/eval_jaxpr/reduce_sum | solution.py:72
  289.6 16.1 %bitcast_dynamic-update-slice_fusion.3 = f32[2,512,2,4,128]{4,1,3,2,0:T(8,128)} fusion(f32[2,512,2,4,128]{4,1,3,2,0:T(8,128)} %get-tuple-element.475, s32[]{:T(128)S(6)} %copy.59, f32[2,512,4,2048]{3,1,2,0:T(8,128)} %get-tuple-element.437, f32[512,2,4]{0,2,1:T(4,128)S(1)} %get-tuple-element.439, pred[512,2048]{1,0:T(8,128)(4,1)S(1)} %fusion.79, ...), kind=kOutput, calls=%fused_computation.14.clone.1 | convolution fusion | flops 2189950976 | bytes 38830084 | tf_op jit(solution)/shard_map/while/body/eval_jaxpr/qgrk,kgd->qgrd/dot_general | solution.py:73
  307.9 15.3 %bitcast_reduce_fusion.4 = (f32[512,2,4]{0,2,1:T(4,128)S(1)}, f32[2,512,4,2048]{3,1,2,0:T(8,128)}) fusion(pred[512,2048]{1,0:T(8,128)(4,1)S(1)} %fusion.79, bf16[2048,2,128]{2,0,1:T(8,128)(2,1)} %get-tuple-element.497, bf16[2,512,2,4,128]{4,1,3,2,0:T(8,128)(2,1)} %get-tuple-element.496, s32[]{:T(128)S(6)} %copy.59), kind=kOutput, calls=%fused_computation.2.clone.1 | convolution fusion | flops 2172645376 | bytes 36716548 | tf_op jit(solution)/shard_map/while/body/eval_jaxpr/qgrd,kgd->qgrk/dot_general | solution.py:64
  323.2 15.6 %fusion.80 = f32[512,2,4]{0,2,1:T(4,128)S(1)} fusion(f32[2,512,4,2048]{3,1,2,0:T(8,128)} %get-tuple-element.437, f32[512,2,4]{0,2,1:T(4,128)S(1)} %get-tuple-element.439, pred[512,2048]{1,0:T(8,128)(4,1)S(1)} %fusion.79), kind=kLoop, calls=%fused_computation.7.clone.1 | loop fusion | flops 41938944 | bytes 34635776 | tf_op jit(solution)/shard_map/while/body/eval_jaxpr/reduce_sum | solution.py:72
  338.8 16.1 %bitcast_dynamic-update-slice_fusion.3 = f32[2,512,2,4,128]{4,1,3,2,0:T(8,128)} fusion(f32[2,512,2,4,128]{4,1,3,2,0:T(8,128)} %get-tuple-element.475, s32[]{:T(128)S(6)} %copy.59, f32[2,512,4,2048]{3,1,2,0:T(8,128)} %get-tuple-element.437, f32[512,2,4]{0,2,1:T(4,128)S(1)} %get-tuple-element.439, pred[512,2048]{1,0:T(8,128)(4,1)S(1)} %fusion.79, ...), kind=kOutput, calls=%fused_computation.14.clone.1 | convolution fusion | flops 2189950976 | bytes 38830084 | tf_op jit(solution)/shard_map/while/body/eval_jaxpr/qgrk,kgd->qgrd/dot_general | solution.py:73
  354.9 102.7 %while.28 = (s32[]{:T(128)}, f32[2,512,2,4]{1,3,2,0:T(4,128)S(1)}, f32[2,512,2,4,128]{4,3,2,1,0:T(4,128)}, f32[2,512,2,4]{1,3,2,0:T(4,128)S(1)}, f32[2,512,2,4]{...) while((s32[]{:T(128)}, f32[2,512,2,4]{1,3,2,0:T(4,128)S(1)}, ...), condition=%wide.region_13.14_spmd.clone, body=%wide.region_10.13_spmd.clone.sunk | while | flops 4410333184 | bytes 117696776 | solution.py:100
  356.6 15.3 %bitcast_reduce_fusion.5 = (f32[512,2,4]{0,2,1:T(4,128)S(1)}, f32[2,512,4,2048]{3,1,2,0:T(8,128)}) fusion(pred[512,2048]{1,0:T(8,128)(4,1)S(1)} %fusion.84, bf16[2048,2,128]{2,0,1:T(8,128)(2,1)} %get-tuple-element.531, bf16[2,512,2,4,128]{4,1,3,2,0:T(8,128)(2,1)} %get-tuple-element.530, s32[]{:T(128)S(6)} %copy.70), kind=kOutput, calls=%fused_computation.38.clone.1 | convolution fusion | flops 2172645376 | bytes 36716548 | tf_op jit(solution)/shard_map/while/body/eval_jaxpr/qgrd,kgd->qgrk/dot_general | solution.py:64
  371.9 15.6 %fusion.86 = f32[512,2,4]{0,2,1:T(4,128)S(1)} fusion(f32[2,512,4,2048]{3,1,2,0:T(8,128)} %get-tuple-element.454, f32[512,2,4]{0,2,1:T(4,128)S(1)} %get-tuple-element.456, pred[512,2048]{1,0:T(8,128)(4,1)S(1)} %fusion.84), kind=kLoop, calls=%fused_computation.43.clone.1 | loop fusion | flops 41938944 | bytes 34635776 | tf_op jit(solution)/shard_map/while/body/eval_jaxpr/reduce_sum | solution.py:72
  387.5 16.1 %fusion.88 = f32[1,512,2,4,128]{4,1,3,2,0:T(8,128)S(1)} fusion(f32[2,512,2,4,128]{4,1,3,2,0:T(8,128)} %get-tuple-element.532, s32[]{:T(128)S(6)} %copy.70, f32[2,512,4,2048]{3,1,2,0:T(8,128)} %get-tuple-element.454, f32[512,2,4]{0,2,1:T(4,128)S(1)} %get-tuple-element.456, pred[512,2048]{1,0:T(8,128)(4,1)S(1)} %fusion.84, ...), kind=kOutput, calls=%fused_computation.52.clone.1 | convolution fusion | flops 2190475264 | bytes 40927236 | tf_op jit(solution)/shard_map/while/body/eval_jaxpr/qgrk,kgd->qgrd/dot_general | solution.py:73
  403.5 2.7 copy_dynamic-update-slice_fusion.2
  407.7 15.3 %bitcast_reduce_fusion.5 = (f32[512,2,4]{0,2,1:T(4,128)S(1)}, f32[2,512,4,2048]{3,1,2,0:T(8,128)}) fusion(pred[512,2048]{1,0:T(8,128)(4,1)S(1)} %fusion.84, bf16[2048,2,128]{2,0,1:T(8,128)(2,1)} %get-tuple-element.531, bf16[2,512,2,4,128]{4,1,3,2,0:T(8,128)(2,1)} %get-tuple-element.530, s32[]{:T(128)S(6)} %copy.70), kind=kOutput, calls=%fused_computation.38.clone.1 | convolution fusion | flops 2172645376 | bytes 36716548 | tf_op jit(solution)/shard_map/while/body/eval_jaxpr/qgrd,kgd->qgrk/dot_general | solution.py:64
  423.0 15.6 %fusion.86 = f32[512,2,4]{0,2,1:T(4,128)S(1)} fusion(f32[2,512,4,2048]{3,1,2,0:T(8,128)} %get-tuple-element.454, f32[512,2,4]{0,2,1:T(4,128)S(1)} %get-tuple-element.456, pred[512,2048]{1,0:T(8,128)(4,1)S(1)} %fusion.84), kind=kLoop, calls=%fused_computation.43.clone.1 | loop fusion | flops 41938944 | bytes 34635776 | tf_op jit(solution)/shard_map/while/body/eval_jaxpr/reduce_sum | solution.py:72
  438.6 16.1 %fusion.88 = f32[1,512,2,4,128]{4,1,3,2,0:T(8,128)S(1)} fusion(f32[2,512,2,4,128]{4,1,3,2,0:T(8,128)} %get-tuple-element.532, s32[]{:T(128)S(6)} %copy.70, f32[2,512,4,2048]{3,1,2,0:T(8,128)} %get-tuple-element.454, f32[512,2,4]{0,2,1:T(4,128)S(1)} %get-tuple-element.456, pred[512,2048]{1,0:T(8,128)(4,1)S(1)} %fusion.84, ...), kind=kOutput, calls=%fused_computation.52.clone.1 | convolution fusion | flops 2190475264 | bytes 40927236 | tf_op jit(solution)/shard_map/while/body/eval_jaxpr/qgrk,kgd->qgrd/dot_general | solution.py:73
  454.7 2.7 copy_dynamic-update-slice_fusion.2
  457.6 5.5 reshape.383
  463.6 3.8 div.30
  467.4 5.5 div.31
  472.9 15.8 %convolution_convert_fusion = bf16[1024,4096]{1,0:T(8,128)(2,1)} fusion(bf16[1024,4096]{1,0:T(8,128)(2,1)} %param.16, f32[1024,1024]{1,0:T(8,128)} %reshape.383, f32[1024,1024]{1,0:T(8,128)} %div.31), kind=kOutput, calls=%fused_computation.74 | convolution fusion | flops 8596226048 | bytes 25165824 | tf_op jit(solution)/shard_map/dot_general | solution.py:227
  488.7 141.9 %reduce-scatter.2.cloned.1.call-done = bf16[256,4096]{1,0:T(8,128)(2,1)} async-done(((bf16[1024,4096]{1,0:T(8,128)(2,1)}), bf16[256,4096]{1,0:T(8,128)(2,1)}) %reduce-scatter.2.cloned.1.call-update) | async-done | bytes 2097168 | tf_op jit(solution)/shard_map/reduce_scatter | solution.py:226
  (93 shorter events, 29.5 us)
Async XLA Ops:
  6.5 5.5 copy-start
  6.5 5.5 copy-start.5
  6.5 27.5 %all-gather.6.cloned.1.call-start = ((), (), s32[]{:S(2)}) async-start(), calls=%async_computation.2 | async-start | bytes 1179648 | tf_op jit(solution)/shard_map/all_gather | solution.py:196
  9.0 50.5 %all-gather.8.cloned.1.call-start = ((), (), s32[]{:S(2)}) async-start(), calls=%async_computation.3 | async-start | bytes 1179648 | tf_op jit(solution)/shard_map/all_gather | solution.py:197
  9.9 4.2 copy-start.4
  9.9 200.9 %all-gather.4.cloned.1.call-start = ((), (), s32[]{:S(2)}) async-start(), calls=%async_computation.1 | async-start | bytes 10485760 | tf_op jit(solution)/shard_map/all_gather | solution.py:127
  14.0 616.6 %reduce-scatter.2.cloned.1.call-start = ((), (), s32[]{:S(2)}) async-start(), calls=%async_computation.4 | async-start | bytes 10485760 | tf_op jit(solution)/shard_map/reduce_scatter | solution.py:226
  14.8 5.0 copy-start.6
  221.1 0.9 copy-start.1
  222.0 30.1 %collective-permute-start = (bf16[1024,2,128]{0,2,1:T(8,128)(2,1)}, bf16[1024,2,128]{0,2,1:T(8,128)(2,1)}, u32[]{:S(2)}, u32[]{:S(2)}) collective-permute-start(bf16[1024,2,128]{0,2,1:T(8,128)(2,1)} %pad_maximum_fusion.2), channel_id=1, source_target_pairs={{0,4},{4,8},{8,12},{12,16},{16,20},{20,24},{24,28},{1,5},{5,9},{9,... | collective-permute-start | bytes 1572872 | tf_op jit(solution)/shard_map/ppermute | solution.py:32
  240.5 14.1 %collective-permute-start.1 = (bf16[1024,2,128]{0,2,1:T(8,128)(2,1)}, bf16[1024,2,128]{0,2,1:T(8,128)(2,1)}, u32[]{:S(2)}, u32[]{:S(2)}) collective-permute-start(bf16[1024,2,128]{0,2,1:T(8,128)(2,1)} %bitcast.191), channel_id=1, source_target_pairs={{0,4},{4,8},{8,12},{12,16},{16,20},{20,24},{24,28},{1,5},{5,9},{9,... | collective-permute-start | bytes 1572872 | tf_op jit(solution)/shard_map/ppermute | solution.py:32
  247.9 6.7 %copy-start.2 = (bf16[1024,1,256]{0,2,1:T(8,128)(2,1)S(1)}, bf16[1024,1,256]{0,2,1:T(8,128)(2,1)}, u32[]{:S(2)}) copy-start(bf16[1024,1,256]{0,2,1:T(8,128)(2,1)} %get-tuple-element.278) | copy-start | bytes 1572868
  256.5 98.4 %copy-start.3 = (s32[16]{0:T(128)S(1)}, s32[16]{0:T(128)}, u32[]{:S(2)}) copy-start(s32[16]{0:T(128)} %broadcast_multiply_fusion) | copy-start | bytes 196
Sparse Core Ops, SparseCore 0:
  9.2 24.7 all-gather.5
  35.9 23.5 all-gather.7
  61.1 149.6 all-gather.3
  488.8 141.7 reduce-scatter.1
where the time goes:
time: 647 us; the launch traced here: 637 us
  waiting for transfers between devices  327 us (51%)
  matrix products  164 us (25%)
  other arithmetic  84.2 us (13%)
  local copies, waits for them, and re-layouts  43 us (7%)
  between operations  13.6 us (2%)
    all_gather x1, waiting for transfers between devices, local(): piece = lax.all_gather(normed, 'tp', axis=0, tiled=True)  149 us
    reduce_scatter x1, waiting for transfers between devices, local(): lax.psum_scatter(jnp.dot(rows, w_out, preferred_element_type=jnp.float32)...  142 us
    dot_general x4, matrix products, fold_block(): jnp.einsum('qgrk,kgd->qgrd', weights.astype(jnp.bfloat16), values, prefer...  64.3 us
    reduce_sum x4, other arithmetic, fold_block(): new_sum = run_sum * factor + jnp.sum(weights, axis=-1)  62.3 us
    dot_general x4, matrix products, fold_block(): jnp.einsum('qgrd,kgd->qgrk', queries, keys, preferred_element_type=jnp.fl...  61.1 us
    all_gather x1, waiting for transfers between devices, local(): piece_values = lax.all_gather(cache_values, 'grp', axis=0, tiled=True)  23.2 us
    dot_general x1, matrix products, local(): jnp.dot(rows, w_out, preferred_element_type=jnp.float32)  15.8 us
    dot_general x1, matrix products, local(): query_part = jnp.dot(piece, w_query, preferred_element_type=jnp.float32)  13.2 us
  transfers between devices with their start and end apart: 6, of which 4 were waited for; matrix products, arithmetic and copies ran while one was open for 7% of the time, Pallas kernels for 0%

commit v1 on v0

v1 whole, which is shorter than its diff:
```python
import functools
import math

import jax
import jax.numpy as jnp
from jax import lax
from jax.experimental import pallas as pl
from jax.experimental.pallas import tpu as pltpu
from jax.sharding import PartitionSpec as P

KVH = 8
HD = 128
SINKS = 4
ROWS = 256
PREFIX_STEP = 512
SUFFIX_STEP = 256
MASKED = -1e30
EXPONENT = math.log2(math.e) * HD ** (-0.5)
VMEM_LIMIT = 48 * 1024 * 1024


def parameters():
    return pltpu.CompilerParams(vmem_limit_bytes=VMEM_LIMIT)


def project_kernel(offsets, x_ref, cos_ref, sin_ref, *refs, turned):
    pieces, out_ref = refs[:-1], refs[-1]
    total = None
    for index, piece in enumerate(pieces):
        depth = piece.shape[0]
        if len(pieces) == 1:
            columns = x_ref[...]
        else:
            columns = x_ref[:, pl.ds(pl.multiple_of(offsets[index], depth), depth)]
        term = jnp.dot(columns, piece[...], preferred_element_type=jnp.float32)
        total = term if total is None else total + term

    def store(rotated):
        for head in range(out_ref.shape[1] // HD):
            where = slice(head * HD, (head + 1) * HD)
            part = total[:, where]
            if rotated:
                part = part * cos_ref[...] + pltpu.roll(part, HD // 2, 1) * sin_ref[...]
            out_ref[:, where] = part.astype(out_ref.dtype)

    pl.when(pl.program_id(0) < turned)(lambda: store(True))
    pl.when(pl.program_id(0) >= turned)(lambda: store(False))


def project(x, pieces, offsets, cosine, sine, turned_columns):
    rows, width = x.shape
    columns = pieces[0].shape[1]
    tile = min(256, columns)

    def whole(*unused):
        return (0, 0)

    return pl.pallas_call(
        functools.partial(project_kernel, turned=turned_columns // tile),
        out_shape=jax.ShapeDtypeStruct((rows, columns), jnp.bfloat16),
        grid_spec=pltpu.PrefetchScalarGridSpec(
            num_scalar_prefetch=1,
            grid=(columns // tile,),
            in_specs=[
                pl.BlockSpec((rows, width), whole),
                pl.BlockSpec((rows, HD), whole),
                pl.BlockSpec((rows, HD), whole),
            ]
            + [pl.BlockSpec((piece.shape[0], tile), lambda j, *_: (0, j)) for piece in pieces],
            out_specs=pl.BlockSpec((rows, tile), lambda j, *_: (0, j)),
        ),
        compiler_params=parameters(),
        cost_estimate=pl.CostEstimate(
            flops=2 * rows * width * columns,
            bytes_accessed=2 * (rows * width + width * columns + rows * columns),
            transcendentals=0,
        ),
        name="project",
    )(offsets, x, cosine, sine, *pieces)


def attend_kernel(
    page_rows, bounds, q_ref, row_ref, pk_ref, pv_ref, *refs, window, spans, page_len, share
):
    suffix_refs = refs[: 2 * spans]
    out_ref, keys, values, highest, total = refs[2 * spans :]
    block = pl.program_id(1)
    prefix_len = pk_ref.shape[0]

    @pl.when(block == 0)
    def fill():
        values[:, HD:] = jnp.ones_like(values[:, HD:])
        for page in range(prefix_len // page_len):
            source = pl.ds(pl.multiple_of(page_rows[page], page_len), page_len)
            target = slice(page * page_len, (page + 1) * page_len)
            keys[target, :] = pk_ref[source, :]
            values[target, :HD] = pv_ref[source, :]
        base = prefix_len
        for span in range(spans):
            key_ref, value_ref = suffix_refs[2 * span : 2 * span + 2]
            size = key_ref.shape[0]
            keys[base : base + size, :] = key_ref[...]
            values[base : base + size, :HD] = value_ref[...]
            base += size

    highest[...] = jnp.full_like(highest, MASKED)
    total[...] = jnp.zeros_like(total)

    def step(base, size, visible):
        for head in range(share):
            queries = q_ref[:, head * HD : (head + 1) * HD]
            scores = lax.dot_general(
                queries,
                keys[pl.ds(base, size), :],
                (((1,), (1,)), ((), ())),
                preferred_element_type=jnp.float32,
            )
            if visible is not None:
                scores = jnp.where(visible, scores, MASKED)
            before = highest[head]
            after = jnp.maximum(before, jnp.max(scores, axis=1, keepdims=True))
            highest[head] = after
            spread = jnp.concatenate([after] * (size // HD), axis=1)
            weights = jnp.exp2((scores - spread) * EXPONENT)
            factor = jnp.exp2((before - after) * EXPONENT)
            total[head] = total[head] * jnp.concatenate([factor, factor], axis=1) + jnp.dot(
                weights.astype(jnp.bfloat16),
                values[pl.ds(base, size), :],
                preferred_element_type=jnp.float32,
            )

    behind_min, behind_max = bounds[4 * block], bounds[4 * block + 1]
    first_min, own_max = bounds[4 * block + 2], bounds[4 * block + 3]
    rows = q_ref.shape[0]

    def prefix_step(index, carry):
        base = pl.multiple_of(index * PREFIX_STEP, PREFIX_STEP)
        last = base + PREFIX_STEP - 1
        unmasked = (base > behind_max) & (last <= behind_min + window)
        unseen = (last <= behind_min) & (base >= SINKS)

        @pl.when(unmasked)
        def plain():
            step(base, PREFIX_STEP, None)

        @pl.when(jnp.logical_not(unmasked | unseen))
        def masked():
            behind = row_ref[:, 0:1]
            place = base + lax.broadcasted_iota(jnp.int32, (rows, PREFIX_STEP), 1)
            visible = ((place > behind) | (place < SINKS)) & (place <= behind + window)
            step(base, PREFIX_STEP, visible)

        return carry

    lax.fori_loop(0, prefix_len // PREFIX_STEP, prefix_step, 0)

    def suffix_step(index, carry):
        base = pl.multiple_of(index * SUFFIX_STEP, SUFFIX_STEP)
        place = base + lax.broadcasted_iota(jnp.int32, (rows, SUFFIX_STEP), 1)
        visible = (place >= row_ref[:, 1:2]) & (place <= row_ref[:, 2:3])
        step(pl.multiple_of(prefix_len + base, SUFFIX_STEP), SUFFIX_STEP, visible)
        return carry

    lax.fori_loop(first_min // SUFFIX_STEP, own_max // SUFFIX_STEP + 1, suffix_step, 0)
    for head in range(share):
        out_ref[:, head * HD : (head + 1) * HD] = (
            total[head][:, :HD] / total[head][:, HD:]
        ).astype(out_ref.dtype)


def attend(queries, row_info, bounds, prefix, page_rows, page_len, suffix, window):
    rows = queries.shape[0]
    kv_heads = prefix.shape[1] // (2 * HD)
    share = queries.shape[1] // (kv_heads * HD)
    prefix_len = prefix.shape[0]
    count = prefix_len + sum(part.shape[0] for part in suffix)

    def key_of(size):
        return pl.BlockSpec((size, HD), lambda h, i, *_: (0, h))

    def value_of(size):
        return pl.BlockSpec((size, HD), lambda h, i, *_: (0, kv_heads + h))

    specs = [
        pl.BlockSpec((ROWS, share * HD), lambda h, i, *_: (i, h)),
        pl.BlockSpec((ROWS, HD), lambda h, i, *_: (i, 0)),
        key_of(prefix_len),
        value_of(prefix_len),
    ]
    operands = [queries, row_info, prefix, prefix]
    for part in suffix:
        specs += [key_of(part.shape[0]), value_of(part.shape[0])]
        operands += [part, part]
    return pl.pallas_call(
        functools.partial(
            attend_kernel, window=window, spans=len(suffix), page_len=page_len, share=share
        ),
        out_shape=jax.ShapeDtypeStruct(queries.shape, jnp.bfloat16),
        grid_spec=pltpu.PrefetchScalarGridSpec(
            num_scalar_prefetch=2,
            grid=(kv_heads, rows // ROWS),
            in_specs=specs,
            out_specs=pl.BlockSpec((ROWS, share * HD), lambda h, i, *_: (i, h)),
            scratch_shapes=[
                pltpu.VMEM((count, HD), jnp.bfloat16),
                pltpu.VMEM((count, 2 * HD), jnp.bfloat16),
                pltpu.VMEM((share, ROWS, HD), jnp.float32),
                pltpu.VMEM((share, ROWS, 2 * HD), jnp.float32),
            ],
        ),
        compiler_params=parameters(),
        cost_estimate=pl.CostEstimate(
            flops=8 * rows * queries.shape[1] * (prefix_len + prefix_len // 4),
            bytes_accessed=2 * (2 * queries.size + 2 * kv_heads * HD * count),
            transcendentals=rows * queries.shape[1] // HD * prefix_len,
        ),
        name="attend",
    )(page_rows, bounds, *operands)


def outward_kernel(offsets, *refs, parts):
    out_ref, full = refs[-2:]
    attn_refs, weights = refs[: len(parts)], refs[len(parts) : -2]
    total = None
    at = 0
    for attn, count in zip(attn_refs, parts):
        if count == 1:
            weight = weights[at][...]
        else:
            for index in range(count):
                piece = weights[at + index]
                depth = piece.shape[0]
                where = pl.ds(pl.multiple_of(offsets[index], depth), depth)
                full[where, :] = piece[...]
            weight = full[...]
        at += count
        term = jnp.dot(attn[...], weight, preferred_element_type=jnp.float32)
        total = term if total is None else total + term
    out_ref[...] = total.astype(out_ref.dtype)


def outward(pairs, offsets):
    rows = pairs[0][0].shape[0]
    columns = pairs[0][1][0].shape[1]
    tile = min(512, columns)
    depth = pairs[-1][0].shape[1]
    attns = [attn for attn, unused in pairs]
    pieces = [piece for unused, stack in pairs for piece in stack]
    return pl.pallas_call(
        functools.partial(outward_kernel, parts=tuple(len(stack) for unused, stack in pairs)),
        out_shape=jax.ShapeDtypeStruct((rows, columns), jnp.bfloat16),
        grid_spec=pltpu.PrefetchScalarGridSpec(
            num_scalar_prefetch=1,
            grid=(columns // tile,),
            in_specs=[pl.BlockSpec(attn.shape, lambda j, *_: (0, 0)) for attn in attns]
            + [pl.BlockSpec((piece.shape[0], tile), lambda j, *_: (0, j)) for piece in pieces],
            out_specs=pl.BlockSpec((rows, tile), lambda j, *_: (0, j)),
            scratch_shapes=[pltpu.VMEM((depth, tile), jnp.bfloat16)],
        ),
        compiler_params=parameters(),
        cost_estimate=pl.CostEstimate(
            flops=2 * rows * columns * depth * len(pairs),
            bytes_accessed=2 * columns * (rows + depth * len(pairs)),
            transcendentals=0,
        ),
        name="outward",
    )(offsets, *attns, *pieces)


def rotation(positions):
    half = HD // 2
    freqs = 500000.0 ** (-jnp.arange(half, dtype=jnp.float32) * 2.0 / HD)
    angles = positions.astype(jnp.float32)[:, None] * freqs[None, :]
    cosine, sine = jnp.cos(angles), jnp.sin(angles)
    return jnp.concatenate([cosine, cosine], axis=1), jnp.concatenate([-sine, sine], axis=1)


def block_bounds(behind, first, own):
    def blocks(array):
        return array.reshape(-1, ROWS)

    return jnp.stack(
        [
            blocks(behind).min(axis=1),
            blocks(behind).max(axis=1),
            blocks(first).min(axis=1),
            blocks(own).max(axis=1),
        ],
        axis=1,
    ).reshape(-1).astype(jnp.int32)


def row_table(behind, first, own):
    rows = behind.shape[0]
    table = jnp.stack([behind, first, own], axis=1).astype(jnp.int32)
    return jnp.concatenate([table, jnp.zeros((rows, HD - 3), jnp.int32)], axis=1)


def normalize(x_rows, norm_gain):
    wide = x_rows.astype(jnp.float32)
    variance = jnp.mean(wide * wide, axis=-1, keepdims=True) + 1e-05
    return (wide * lax.rsqrt(variance) * norm_gain).astype(jnp.bfloat16)


def first_of_request(request_ids, wanted, count):
    labels = jnp.arange(count, dtype=jnp.int32)
    counts = jnp.sum((request_ids[:, None] == labels[None, :]).astype(jnp.int32), axis=0)
    starts = jnp.cumsum(counts) - counts
    match = wanted[:, None] == labels[None, :]
    return jnp.sum(jnp.where(match, starts[None, :], 0), axis=1)


def join_pair(lower, mine, peer):
    return jnp.where(
        lower, jnp.concatenate([mine, peer], axis=2), jnp.concatenate([peer, mine], axis=2)
    )


def swapped(block, axis, apart):
    route = [(i, i ^ 1 << apart) for i in range(lax.axis_size(axis))]
    return lax.ppermute(block, axis, route)


def shifted(block, axis, distance):
    route = [(i, i + distance) for i in range(lax.axis_size(axis) - distance)]
    return lax.ppermute(block, axis, route)


def by_heads(x_rows, norm_gain, w_query, w_keyval, w_out, prefix_cache, page_table, request_ids):
    tp_size = lax.axis_size("tp")
    grp_size = lax.axis_size("grp")
    tp_index = lax.axis_index("tp")
    grp_index = lax.axis_index("grp")
    tok_group = x_rows.shape[0] * tp_size
    kv_cols = w_keyval.shape[2]
    kv_need = max(HD, HD * KVH // tp_size)
    pages_dev, page_len = prefix_cache.shape[:2]
    prefix_len = pages_dev * grp_size * page_len
    pair_bits = (kv_need // kv_cols).bit_length() - 1
    no_offsets = jnp.zeros((1,), jnp.int32)

    normed = normalize(x_rows, norm_gain)
    tokens = lax.all_gather(normed, "tp", axis=0, tiled=True)
    group_start = grp_index * tok_group
    token_index = group_start + jnp.arange(tok_group, dtype=jnp.int32)
    own_seg = lax.dynamic_slice_in_dim(request_ids, group_start, tok_group, 0)
    own_first = first_of_request(request_ids, own_seg, 2 * grp_size)
    own_pos = prefix_len + token_index - own_first
    cosine, sine = rotation(own_pos)
    queries = project(tokens, [w_query], no_offsets, cosine, sine, w_query.shape[1])
    kv_weight = w_keyval.reshape(w_keyval.shape[0], 2 * kv_cols)
    cache = prefix_cache.reshape(pages_dev * page_len, 2, kv_cols)
    if pair_bits == 0:
        own = project(tokens, [kv_weight], no_offsets, cosine, sine, kv_cols)
    else:
        keyval = jnp.dot(tokens, kv_weight, preferred_element_type=jnp.float32)
        keyval = keyval.astype(jnp.bfloat16).reshape(tok_group, 2, kv_cols)
        for bit_num in range(pair_bits):
            lower = tp_index >> bit_num & 1 == 0
            keyval = join_pair(lower, keyval, swapped(keyval, "tp", bit_num))
            cache = join_pair(lower, cache, swapped(cache, "tp", bit_num))
        keys = keyval[:, 0].astype(jnp.float32).reshape(tok_group, -1, HD)
        keys = keys * cosine[:, None] + jnp.roll(keys, HD // 2, axis=2) * sine[:, None]
        keys = keys.reshape(tok_group, kv_need).astype(jnp.bfloat16)
        own = jnp.concatenate([keys, keyval[:, 1]], axis=1)
    before = shifted(own, "grp", 1)
    cache = cache.reshape(pages_dev * page_len, 2 * kv_need)
    prefix = lax.all_gather(cache, "grp", axis=0, tiled=True)
    behind = own_pos - prefix_len
    place = tok_group + jnp.arange(tok_group, dtype=jnp.int32)
    first = jnp.maximum(own_first - group_start + tok_group, place - prefix_len + 1)
    attn = attend(
        queries,
        row_table(behind, first, place),
        block_bounds(behind, first, place),
        prefix,
        page_table * page_len,
        page_len,
        [before, own],
        prefix_len,
    )
    return lax.psum_scatter(
        outward([(attn, [w_out])], no_offsets), "tp", scatter_dimension=0, tiled=True
    )


def solution(mesh):
    placed = (
        P(("grp", "tp"), None),
        P(),
        P(None, "tp"),
        P(None, None, "tp"),
        P("tp", None),
        P("grp", None, None, "tp"),
        P(),
        P(),
    )
    return jax.shard_map(
        by_heads, mesh=mesh, in_specs=placed, out_specs=P(("grp", "tp"), None), check_vma=False
    )
```

time: 647 us -> 424 us (0.66); the launches traced: 637 us -> 422 us
  matrix products: 164 us -> 0 us
  Pallas kernels: 0 us -> 92.8 us
  other arithmetic: 84.2 us -> 11.4 us
  local copies, waits for them, and re-layouts: 43 us -> 7.55 us
  waiting for transfers between devices: 327 us -> 295 us
    dot_general x11 -> x0, matrix products: 164 us -> none  [the longest x4 64.3 us: fold_block(): jnp.einsum('qgrk,kgd->qgrd', weights.astype(jnp.bfloat16), values, prefer...]
    pallas_call x0 -> x4, Pallas kernels: none -> 92.8 us  [the longest x1 55 us: attend(): pl.pallas_call(functools.partial(attend_kernel, window=window, spans=len(...]
    reduce_sum x8 -> x3, other arithmetic: 64.8 us -> 2.39 us  [the longest x1 2.13 us: normalize(): variance = jnp.mean(wide * wide, axis=-1, keepdims=True) + 1e-05]
    all_gather x3 -> x2, waiting for transfers between devices: 185 us -> 141 us  [the longest x1 141 us: by_heads(): tokens = lax.all_gather(normed, 'tp', axis=0, tiled=True)]
    reduce_scatter x1, waiting for transfers between devices: 142 us -> 152 us  [by_heads(): lax.psum_scatter(outward([(attn, [w_out])], no_offsets), 'tp', scatter_di...]
    div x3 -> x0, local copies, waits for them, and re-layouts: 9.84 us -> none  [local(): state[2] / state[1][..., None]]
    and x4 -> x0, other arithmetic: 6.89 us -> none  [the longest x2 4.26 us: suffix_visible(): same & ((query_pos[:, None] - suffix_pos[None, :] < prefix_len) | (suffix...]
  transfers between devices with their start and end apart: 6 -> 4, of which waited for: 4 -> 4; matrix products, arithmetic and copies ran while one was open for 7% -> 3% of each run, Pallas kernels for 0% -> 6%
where the time goes in v1:
time: 424 us; the launch traced here: 422 us
  waiting for transfers between devices  295 us (70%)
  Pallas kernels  92.8 us (22%)
  between operations  13.3 us (3%)
  other arithmetic  11.4 us (3%)
  local copies, waits for them, and re-layouts  7.55 us (2%)
    reduce_scatter x1, waiting for transfers between devices, by_heads(): lax.psum_scatter(outward([(attn, [w_out])], no_offsets), 'tp', scatter_di...  152 us
    all_gather x1, waiting for transfers between devices, by_heads(): tokens = lax.all_gather(normed, 'tp', axis=0, tiled=True)  141 us
    pallas_call x1, Pallas kernels, attend(): pl.pallas_call(functools.partial(attend_kernel, window=window, spans=len(...  55 us
    pallas_call x2, Pallas kernels, project(): pl.pallas_call(functools.partial(project_kernel, turned=turned_columns //...  24.2 us
    pallas_call x1, Pallas kernels, outward(): pl.pallas_call(functools.partial(outward_kernel, parts=tuple((len(stack)...  13.5 us
  transfers between devices with their start and end apart: 4, of which 4 were waited for; matrix products, arithmetic and copies ran while one was open for 3% of the time, Pallas kernels for 6%

profile of v1, /device:TPU:2, one launch (start us, length us, event | category | flops | bytes accessed | tf_op | source)
XLA Modules:
  0.0 421.8 jit_solution(13118882683676204757)
XLA Ops:
  6.5 2.1 fusion
  8.7 3.5 fusion.2
  12.2 0.0 all-gather.3.cloned.1.call-update
  12.2 0.0 all-gather.5.cloned.1.call-start
  12.3 0.7 copy.28
  13.0 0.0 all-gather.5.cloned.1.call-update
  13.1 0.0 reduce-scatter.2.cloned.1.call-start
  13.1 0.2 convert_reduce_fusion
  13.3 0.1 copy.19
  13.4 0.1 reduce
  13.6 4.9 %copy.29 = bf16[512,8,2,256]{3,1,2,0:T(8,128)(2,1)} copy(bf16[512,8,2,256]{3,2,1,0:T(2,128)(2,1)} %bitcast.11) | data formatting | bytes 8388608
  18.5 0.1 select_reduce_fusion
  18.6 0.2 copy.22
  18.8 0.1 add_reduce_fusion
  19.0 0.2 fusion.5
  19.2 1.9 fusion.3
  21.1 0.3 pad_maximum_fusion
  21.5 1.2 subtract_add_fusion
  22.6 140.7 %all-gather.3.cloned.1.call-done.x_ref = bf16[1024,4096]{1,0:T(8,128)(2,1)} async-done(((bf16[256,4096]{1,0:T(8,128)(2,1)}), bf16[1024,4096]{1,0:T(8,128)(2,1)}) %all-gather.3.cloned.1.call-update) | async-done | bytes 8388624 | tf_op jit(solution)/shard_map/all_gather | solution.py:343
  163.3 9.2 %project.3.refs_2_.refs_3_ = bf16[1024,512]{1,0:T(8,128)(2,1)S(1)} custom-call(s32[1]{0:T(128)} %constant.18.clone.1.offsets, bf16[1024,4096]{1,0:T(8,128)(2,1)} %all-gather.3.cloned.1.call-done.x_ref, f32[1024,128]{1,0:T(8,128)S(1)} %get-tuple-element.13.cos_ref, f32[1024,128]{1,0:T(8,128)S(1)} %get-tuple-element.14.sin_ref, bf16[4096,512]{1,0:T(8,128)(2,1)} %bitcast.12), custom_call_target="tpu_custom_call" | custom-call | flops 4294967296 | bytes 13631488 | tf_op jit(solution)/shard_map/project/pallas_call | solution.py:58
  172.5 2.1 collective-permute-start
  174.6 0.1 copy.20
  174.7 0.1 reshape.116.bounds
  174.8 0.1 pad.3.clone
  174.9 1.5 add_add_fusion.row_ref
  176.5 15.0 %project.2.q_ref = bf16[1024,1024]{1,0:T(8,128)(2,1)S(1)} custom-call(s32[1]{0:T(128)} %constant.18.clone.1.offsets, bf16[1024,4096]{1,0:T(8,128)(2,1)} %all-gather.3.cloned.1.call-done.x_ref, f32[1024,128]{1,0:T(8,128)S(1)} %get-tuple-element.13.cos_ref, f32[1024,128]{1,0:T(8,128)S(1)} %get-tuple-element.14.sin_ref, bf16[4096,1024]{1,0:T(8,128)(2,1)} %refs_0_.1), custom_call_target="tpu_custom_call" | custom-call | flops 8589934592 | bytes 18874368 | tf_op jit(solution)/shard_map/project/pallas_call | solution.py:58
  191.5 1.3 copy-done
  192.8 0.6 all-gather.5.cloned.1.call-done.pk_ref.pv_ref
  193.4 0.9 collective-permute-done.refs_0_.refs_1_
  194.3 55.0 %attend.1.refs_0_ = bf16[1024,1024]{1,0:T(8,128)(2,1)S(1)} custom-call(s32[16]{0:T(128)S(1)} %broadcast_multiply_fusion.page_rows, s32[16]{0:T(128)S(1)} %reshape.116.bounds, bf16[1024,1024]{1,0:T(8,128)(2,1)} %copy-done, s32[1024,128]{1,0:T(8,128)S(1)} %add_add_fusion.row_ref, bf16[2048,512]{1,0:T(8,128)(2,1)} %all-gather.5.cloned.1.call-done.pk_ref.pv_ref, ...), custom_call_target="tpu_custom_call" | custom-call | flops 21474836480 | bytes 8388608 | tf_op jit(solution)/shard_map/attend/pallas_call | solution.py:194
  249.3 13.5 %outward.1 = bf16[1024,4096]{1,0:T(8,128)(2,1)} custom-call(s32[1]{0:T(128)} %constant.18.clone.1.offsets, bf16[1024,1024]{1,0:T(8,128)(2,1)S(1)} %attend.1.refs_0_, bf16[1024,4096]{1,0:T(8,128)(2,1)} %refs_1_.1), custom_call_target="tpu_custom_call" | custom-call | flops 8589934592 | bytes 16777216 | tf_op jit(solution)/shard_map/outward/pallas_call | solution.py:249
  262.9 152.4 %reduce-scatter.2.cloned.1.call-done = bf16[256,4096]{1,0:T(8,128)(2,1)} async-done(((bf16[1024,4096]{1,0:T(8,128)(2,1)}), bf16[256,4096]{1,0:T(8,128)(2,1)}) %reduce-scatter.2.cloned.1.call-update) | async-done | bytes 2097168 | tf_op jit(solution)/shard_map/reduce_scatter | solution.py:382
  (21 shorter events, 0.2 us)
Async XLA Ops:
  6.5 5.8 %copy-start.1 = (bf16[2,128,2,256]{3,2,1,0:T(2,128)(2,1)S(1)}, bf16[2,128,2,256]{3,2,1,0:T(2,128)(2,1)}, u32[]{:S(2)}) copy-start(bf16[2,128,2,256]{3,2,1,0:T(2,128)(2,1)} %param.13) | copy-start | bytes 786436
  6.5 6.6 %copy-start.2 = (s32[8192]{0:T(1024)S(1)}, s32[8192]{0:T(1024)}, u32[]{:S(2)}) copy-start(s32[8192]{0:T(1024)} %param.15) | copy-start | bytes 98308
  6.5 156.7 %all-gather.3.cloned.1.call-start = ((), (), s32[]{:S(2)}) async-start(), calls=%async_computation.1 | async-start | bytes 10485760 | tf_op jit(solution)/shard_map/all_gather | solution.py:343
  12.2 181.1 %all-gather.5.cloned.1.call-start = ((), (), s32[]{:S(2)}) async-start(), calls=%async_computation.2 | async-start | bytes 2359296 | tf_op jit(solution)/shard_map/all_gather | solution.py:368
  13.1 402.2 %reduce-scatter.2.cloned.1.call-start = ((), (), s32[]{:S(2)}) async-start(), calls=%async_computation.3 | async-start | bytes 10485760 | tf_op jit(solution)/shard_map/reduce_scatter | solution.py:382
  13.6 4.9 %dynamic-slice-start = ((s32[8192]{0:T(1024)}, s32[]{:T(128)}), s32[1024]{0:T(1024)S(1)}, s32[]{:S(2)}) async-start(s32[8192]{0:T(1024)} %param.15, s32[]{:T(128)} %select_n.7), calls=%async_computation.4 | async-start | bytes 8704 | tf_op jit(solution)/shard_map/dynamic_slice | solution.py:346
  18.5 2.9 copy-start.3
  172.5 21.8 %collective-permute-start = (bf16[1024,512]{1,0:T(8,128)(2,1)S(1)}, bf16[1024,512]{1,0:T(8,128)(2,1)}, u32[]{:S(2)}, u32[]{:S(2)}) collective-permute-start(bf16[1024,512]{1,0:T(8,128)(2,1)S(1)} %project.3.refs_2_.refs_3_), channel_id=1, source_target_pairs={{0,4},{4,8},{8,12},{12,16},{16,20},{20,24},{24,28},{1,5},{5,9},{9,... | collective-permute-start | bytes 3145736 | tf_op jit(solution)/shard_map/ppermute | solution.py:326
  191.5 1.3 copy-start
Sparse Core Ops, SparseCore 0:
  12.4 150.8 all-gather.2
  165.2 28.1 all-gather.4
  263.0 152.2 reduce-scatter.1

commit v2 on v1

--- a/solution.py
+++ b/solution.py
@@ -168,24 +168,27 @@
         ).astype(out_ref.dtype)
 
 
-def attend(queries, row_info, bounds, prefix, page_rows, page_len, suffix, window):
+def attend(
+    queries, row_info, bounds, prefix, page_rows, page_len, suffix, window, prefix_column=0
+):
     rows = queries.shape[0]
-    kv_heads = prefix.shape[1] // (2 * HD)
+    kv_heads = suffix[0].shape[1] // (2 * HD)
+    skip = prefix_column // HD
     share = queries.shape[1] // (kv_heads * HD)
     prefix_len = prefix.shape[0]
     count = prefix_len + sum(part.shape[0] for part in suffix)
 
-    def key_of(size):
-        return pl.BlockSpec((size, HD), lambda h, i, *_: (0, h))
-
-    def value_of(size):
-        return pl.BlockSpec((size, HD), lambda h, i, *_: (0, kv_heads + h))
+    def key_of(size, at=0):
+        return pl.BlockSpec((size, HD), lambda h, i, *_: (0, at + h))
+
+    def value_of(size, at=0):
+        return pl.BlockSpec((size, HD), lambda h, i, *_: (0, at + kv_heads + h))
 
     specs = [
         pl.BlockSpec((ROWS, share * HD), lambda h, i, *_: (i, h)),
         pl.BlockSpec((ROWS, HD), lambda h, i, *_: (i, 0)),
-        key_of(prefix_len),
-        value_of(prefix_len),
+        key_of(prefix_len, skip),
+        value_of(prefix_len, skip),
     ]
     operands = [queries, row_info, prefix, prefix]
     for part in suffix:
@@ -368,7 +371,8 @@
     prefix = lax.all_gather(cache, "grp", axis=0, tiled=True)
     behind = own_pos - prefix_len
     place = tok_group + jnp.arange(tok_group, dtype=jnp.int32)
-    first = jnp.maximum(own_first - group_start + tok_group, place - prefix_len + 1)
+    first = own_first - group_start + tok_group
+    first = jnp.maximum(jnp.maximum(first, place - prefix_len + 1), 0)
     attn = attend(
         queries,
         row_table(behind, first, place),
@@ -384,7 +388,107 @@
     )
 
 
+def by_pairs(x_rows, norm_gain, w_query, w_keyval, w_out, prefix_cache, page_table, request_ids):
+    grp_size = lax.axis_size("grp")
+    tp_size = lax.axis_size("tp")
+    grp_index = lax.axis_index("grp")
+    tp_index = lax.axis_index("tp")
+    rows, width = x_rows.shape
+    kv_cols = w_keyval.shape[2]
+    pages_dev, page_len = prefix_cache.shape[:2]
+    prefix_len = pages_dev * grp_size * page_len
+    half = 2 * rows
+    no_offsets = jnp.zeros((1,), jnp.int32)
+    owners = grp_index ^ jnp.arange(grp_size, dtype=jnp.int32)
+
+    def across(block, distance):
+        return lax.ppermute(block, "tp", [(i, i ^ distance) for i in range(tp_size)])
+
+    def within(block, distance):
+        return lax.ppermute(block, "grp", [(i, i ^ distance) for i in range(grp_size)])
+
+    def spread(block):
+        blocks = [block] + [within(block, distance) for distance in range(2, grp_size, 2)]
+        return [piece for block in blocks for piece in (block, within(block, 1))]
+
+    def share_of(weight):
+        part = weight.shape[0] // grp_size
+        return lax.dynamic_slice_in_dim(weight, grp_index * part, part, 0)
+
+    def later(block, by):
+        route = []
+        for place in range(2 * grp_size - by):
+            target = place + by
+            for side in range(2):
+                route.append(
+                    (place // 2 * tp_size + place % 2 * 2 + side, target // 2 * tp_size + target % 2 * 2 + side)
+                )
+        return lax.ppermute(block, ("grp", "tp"), route)
+
+    far_cache = across(prefix_cache.reshape(pages_dev * page_len, 2 * kv_cols), 2)
+    far_keyval = across(share_of(w_keyval).reshape(width // grp_size, 2 * kv_cols), 2)
+    normed = normalize(x_rows, norm_gain)
+    peer = across(normed, 1)
+    far_query = across(share_of(w_query), 2)
+    far_keyval = spread(far_keyval)
+    near_cache = prefix_cache.reshape(pages_dev * page_len, 2 * kv_cols)
+    prefix = jnp.concatenate(
+        spread(jnp.concatenate([near_cache, far_cache], axis=1)), axis=0
+    )
+    far_query = spread(far_query)
+    far_out = spread(across(share_of(w_out), 2))
+
+    half_start = grp_index * rows * tp_size + tp_index // 2 * half
+
+    def table_of(plane):
+        place = half + half + plane % 2 * rows + jnp.arange(rows, dtype=jnp.int32)
+        index = half_start - 2 * half + place
+        segments = lax.dynamic_slice_in_dim(request_ids, half_start + plane % 2 * rows, rows, 0)
+        start = first_of_request(request_ids, segments, 2 * grp_size)
+        behind = index - start
+        first = start - half_start + 2 * half
+        first = jnp.maximum(jnp.maximum(first, place - prefix_len + 1), 0)
+        turn = rotation(prefix_len + index - start)
+        return turn, row_table(behind, first, place), block_bounds(behind, first, place)
+
+    own_turn, *own_rows = table_of(tp_index)
+    peer_turn, *peer_rows = table_of(tp_index ^ 1)
+    near_keyval = [w_keyval.reshape(width, 2 * kv_cols)]
+    far_offsets = owners * (width // grp_size)
+
+    def keyval_of(weights, offsets):
+        own = project(normed, weights, offsets, *own_turn, kv_cols)
+        other = project(peer, weights, offsets, *peer_turn, kv_cols)
+        even = tp_index % 2 == 0
+        return jnp.concatenate([jnp.where(even, own, other), jnp.where(even, other, own)], axis=0)
+
+    near = keyval_of(near_keyval, no_offsets)
+    far = keyval_of(far_keyval, far_offsets)
+    near_suffix = [later(near, 2), later(far, 1), near]
+    far_suffix = [later(far, 2), later(near, 1), far]
+    page_owner = page_table // pages_dev
+    page_rows = ((page_owner ^ grp_index) * pages_dev + page_table % pages_dev) * page_len
+
+    def attend_to(tokens, turn, info, weights, offsets, suffix, column):
+        queries = project(tokens, weights, offsets, *turn, w_query.shape[1])
+        return attend(
+            queries, *info, prefix, page_rows, page_len, suffix, prefix_len, prefix_column=column
+        )
+
+    def output_of(tokens, turn, info):
+        near_attn = attend_to(tokens, turn, info, [w_query], no_offsets, near_suffix, 0)
+        far_attn = attend_to(tokens, turn, info, far_query, far_offsets, far_suffix, 2 * kv_cols)
+        return outward(
+            [(near_attn, [w_out]), (far_attn, far_out)], owners * (w_out.shape[0] // grp_size)
+        )
+
+    received = across(output_of(peer, peer_turn, peer_rows), 1)
+    kept = output_of(normed, own_turn, own_rows)
+    return (kept.astype(jnp.float32) + received.astype(jnp.float32)).astype(jnp.bfloat16)
+
+
 def solution(mesh):
+    pairs = mesh.shape["tp"] == 4 and mesh.shape["grp"] == 8
     placed = (
         P(("grp", "tp"), None),
         P(),
@@ -396,5 +500,9 @@
         P(),
     )
     return jax.shard_map(
-        by_heads, mesh=mesh, in_specs=placed, out_specs=P(("grp", "tp"), None), check_vma=False
+        by_pairs if pairs else by_heads,
+        mesh=mesh,
+        in_specs=placed,
+        out_specs=P(("grp", "tp"), None),
+        check_vma=False,
     )

time: 424 us -> 397 us (0.936)
  waiting for transfers between devices: 295 us -> 159 us
  starting transfers between devices: 2.23 us -> 55.3 us
  Pallas kernels: 92.8 us -> 134 us
  local copies, waits for them, and re-layouts: 7.55 us -> 29.8 us
  between operations: 13.3 us -> 0.64 us
  other arithmetic: 11.4 us -> 16.6 us
    ppermute x1 -> x38, waiting for transfers between devices: 0.93 us -> 159 us  [the longest x6 77 us: across(): lax.ppermute(block, 'tp', [(i, i ^ distance) for i in range(tp_size)])]
    reduce_scatter x1 -> x0, waiting for transfers between devices: 152 us -> none  [by_heads(): lax.psum_scatter(outward([(attn, [w_out])], no_offsets), 'tp', scatter_di...]
    all_gather x2 -> x0, waiting for transfers between devices: 141 us -> none  [the longest x1 141 us: by_heads(): tokens = lax.all_gather(normed, 'tp', axis=0, tiled=True)]
    ppermute x1 -> x38, starting transfers between devices: 2.14 us -> 55.3 us  [the longest x28 33.6 us: within(): lax.ppermute(block, 'grp', [(i, i ^ distance) for i in range(grp_size)])]
    pallas_call x2 -> x8, Pallas kernels: 24.2 us -> 42.4 us  [project(): pl.pallas_call(functools.partial(project_kernel, turned=turned_columns //...]
    pallas_call x1 -> x4, Pallas kernels: 55 us -> 68.9 us  [attend(): pl.pallas_call(functools.partial(attend_kernel, window=window, spans=len(...]
    unnamed x10 -> x56, local copies, waits for them, and re-layouts: 6.96 us -> 19.6 us
    pallas_call x1 -> x2, Pallas kernels: 13.5 us -> 22.7 us  [outward(): pl.pallas_call(functools.partial(outward_kernel, parts=tuple((len(stack)...]
  transfers between devices with their start and end apart: 4 -> 38, of which waited for: 4 -> 15; matrix products, arithmetic and copies ran while one was open for 3% -> 10% of each run, Pallas kernels for 6% -> 31%
where the time goes in v2:
time: 397 us; the launch traced here: 395 us
  waiting for transfers between devices  159 us (40%)
  Pallas kernels  134 us (34%)
  starting transfers between devices  55.3 us (14%)
  local copies, waits for them, and re-layouts  29.8 us (8%)
  other arithmetic  16.6 us (4%)
    ppermute x6, waiting for transfers between devices, across(): lax.ppermute(block, 'tp', [(i, i ^ distance) for i in range(tp_size)])  77 us
    pallas_call x4, Pallas kernels, attend(): pl.pallas_call(functools.partial(attend_kernel, window=window, spans=len(...  68.9 us
    ppermute x28, waiting for transfers between devices, within(): lax.ppermute(block, 'grp', [(i, i ^ distance) for i in range(grp_size)])  64.4 us
    pallas_call x8, Pallas kernels, project(): pl.pallas_call(functools.partial(project_kernel, turned=turned_columns //...  42.4 us
    ppermute x28, starting transfers between devices, within(): lax.ppermute(block, 'grp', [(i, i ^ distance) for i in range(grp_size)])  33.6 us
    pallas_call x2, Pallas kernels, outward(): pl.pallas_call(functools.partial(outward_kernel, parts=tuple((len(stack)...  22.7 us
    unnamed x56, local copies, waits for them, and re-layouts  19.6 us
    ppermute x4, waiting for transfers between devices, later(): return lax.ppermute(block, ('grp', 'tp'), route)  17.1 us
  transfers between devices with their start and end apart: 38, of which 15 were waited for; matrix products, arithmetic and copies ran while one was open for 10% of the time, Pallas kernels for 31%

profile of v2, /device:TPU:2, one launch (start us, length us, event | category | flops | bytes accessed | tf_op | source)
XLA Modules:
  0.0 394.9 jit_solution(5038693881863811380)
XLA Ops:
  1.0 2.7 collective-permute-start
  12.2 15.8 %collective-permute-done = bf16[256,512]{1,0:T(8,128)(2,1)S(1)} collective-permute-done((bf16[256,512]{1,0:T(8,128)(2,1)S(1)}, bf16[256,512]{1,0:T(8,128)(2,1)S(1)}, u32[]{:S(2)}, u32[]{:S(2)}) %collective-permute-start) | collective-permute-done | bytes 262176 | tf_op jit(solution)/shard_map/ppermute | solution.py:405
  32.7 5.5 %collective-permute-done.10.refs_0_ = bf16[512,512]{1,0:T(8,128)(2,1)} collective-permute-done((bf16[512,512]{1,0:T(8,128)(2,1)S(1)}, bf16[512,512]{1,0:T(8,128)(2,1)}, u32[]{:S(2)}, u32[]{:S(2)}) %collective-permute-start.10) | collective-permute-done | bytes 524320 | tf_op jit(solution)/shard_map/ppermute | solution.py:405
  42.0 2.9 collective-permute-done.6
  45.0 11.1 %collective-permute-done.4 = bf16[256,1024]{1,0:T(8,128)(2,1)} collective-permute-done((bf16[256,1024]{1,0:T(8,128)(2,1)}, bf16[256,1024]{1,0:T(8,128)(2,1)}, u32[]{:S(2)}, u32[]{:S(2)}) %collective-permute-start.4) | collective-permute-done | bytes 524320 | tf_op jit(solution)/shard_map/ppermute | solution.py:408
  58.1 9.3 %collective-permute-done.16.refs_6_ = bf16[512,512]{1,0:T(8,128)(2,1)} collective-permute-done((bf16[512,512]{1,0:T(8,128)(2,1)}, bf16[512,512]{1,0:T(8,128)(2,1)}, u32[]{:S(2)}, u32[]{:S(2)}) %collective-permute-start.16) | collective-permute-done | bytes 524320 | tf_op jit(solution)/shard_map/ppermute | solution.py:408
  69.2 6.3 %collective-permute-done.14.refs_4_ = bf16[512,512]{1,0:T(8,128)(2,1)} collective-permute-done((bf16[512,512]{1,0:T(8,128)(2,1)}, bf16[512,512]{1,0:T(8,128)(2,1)}, u32[]{:S(2)}, u32[]{:S(2)}) %collective-permute-start.14) | collective-permute-done | bytes 524320 | tf_op jit(solution)/shard_map/ppermute | solution.py:408
  78.8 35.3 %collective-permute-done.29.refs_3_ = bf16[128,4096]{1,0:T(8,128)(2,1)S(1)} collective-permute-done((bf16[128,4096]{1,0:T(8,128)(2,1)}, bf16[128,4096]{1,0:T(8,128)(2,1)S(1)}, u32[]{:S(2)}, u32[]{:S(2)}) %collective-permute-start.29) | collective-permute-done | bytes 1048608 | tf_op jit(solution)/shard_map/ppermute | solution.py:405
  114.1 20.4 %collective-permute-done.19.refs_0_ = bf16[512,1024]{1,0:T(8,128)(2,1)} collective-permute-done((bf16[512,1024]{1,0:T(8,128)(2,1)}, bf16[512,1024]{1,0:T(8,128)(2,1)}, u32[]{:S(2)}, u32[]{:S(2)}) %collective-permute-start.19) | collective-permute-done | bytes 1048608 | tf_op jit(solution)/shard_map/ppermute | solution.py:405
  141.1 4.9 %copy.28 = bf16[512,8,2,256]{3,1,2,0:T(8,128)(2,1)} copy(bf16[512,8,2,256]{3,2,1,0:T(2,128)(2,1)} %bitcast.24) | data formatting | bytes 8388608
  150.2 3.2 project.9
  155.3 6.3 %collective-permute-done.35.refs_9_ = bf16[128,4096]{1,0:T(8,128)(2,1)} collective-permute-done((bf16[128,4096]{1,0:T(8,128)(2,1)S(1)}, bf16[128,4096]{1,0:T(8,128)(2,1)}, u32[]{:S(2)}, u32[]{:S(2)}) %collective-permute-start.35) | collective-permute-done | bytes 1048608 | tf_op jit(solution)/shard_map/ppermute | solution.py:408
  162.3 21.8 %collective-permute-done.33.refs_7_ = bf16[128,4096]{1,0:T(8,128)(2,1)} collective-permute-done((bf16[128,4096]{1,0:T(8,128)(2,1)S(1)}, bf16[128,4096]{1,0:T(8,128)(2,1)}, u32[]{:S(2)}, u32[]{:S(2)}) %collective-permute-start.33) | collective-permute-done | bytes 1048608 | tf_op jit(solution)/shard_map/ppermute | solution.py:408
  184.1 18.1 %collective-permute-start.21 = (bf16[512,1024]{1,0:T(8,128)(2,1)}, bf16[512,1024]{1,0:T(8,128)(2,1)S(1)}, u32[]{:S(2)}, u32[]{:S(2)}) collective-permute-start(bf16[512,1024]{1,0:T(8,128)(2,1)} %collective-permute-done.19.refs_0_), channel_id=1, source_target_pairs={{0,8},{4,12},{8,0},{12,4},{16,24},{20,28},{24,16},{28,20},{1,9},{5... | collective-permute-start | bytes 3145736 | tf_op jit(solution)/shard_map/ppermute | solution.py:408
  207.9 4.4 %project.11 = bf16[256,512]{1,0:T(8,128)(2,1)S(1)} custom-call(s32[8]{0:T(128)S(1)} %fusion.13.offsets, bf16[256,4096]{1,0:T(8,128)(2,1)} %copy-done, f32[256,128]{1,0:T(8,128)S(1)} %pad_maximum_fusion.2.cos_ref, f32[256,128]{1,0:T(8,128)S(1)} %pad_maximum_fusion.3.sin_ref, bf16[512,512]{1,0:T(8,128)(2,1)} %collective-permute-done.10.refs_0_, ...), custom_call_target="tpu_custom_call" | custom-call | flops 1073741824 | bytes 6553600 | tf_op jit(solution)/shard_map/project/pallas_call | solution.py:58
  212.4 4.4 %project.12 = bf16[256,512]{1,0:T(8,128)(2,1)S(1)} custom-call(s32[8]{0:T(128)S(1)} %fusion.13.offsets, bf16[256,4096]{1,0:T(8,128)(2,1)} %collective-permute-done.8.x_ref, f32[256,128]{1,0:T(8,128)S(1)} %pad_maximum_fusion.4.cos_ref, f32[256,128]{1,0:T(8,128)S(1)} %copy-done.4, bf16[512,512]{1,0:T(8,128)(2,1)} %collective-permute-done.10.refs_0_, ...), custom_call_target="tpu_custom_call" | custom-call | flops 1073741824 | bytes 6553600 | tf_op jit(solution)/shard_map/project/pallas_call | solution.py:58
  221.3 4.4 %collective-permute-done.23.refs_4_ = bf16[512,1024]{1,0:T(8,128)(2,1)S(1)} collective-permute-done((bf16[512,1024]{1,0:T(8,128)(2,1)}, bf16[512,1024]{1,0:T(8,128)(2,1)S(1)}, u32[]{:S(2)}, u32[]{:S(2)}) %collective-permute-start.23) | collective-permute-done | bytes 1048608 | tf_op jit(solution)/shard_map/ppermute | solution.py:408
  227.8 4.2 %project.10 = bf16[256,512]{1,0:T(8,128)(2,1)S(1)} custom-call(s32[1]{0:T(128)} %constant.113.clone.1.offsets, bf16[256,4096]{1,0:T(8,128)(2,1)} %collective-permute-done.8.x_ref, f32[256,128]{1,0:T(8,128)S(1)} %pad_maximum_fusion.4.cos_ref, f32[256,128]{1,0:T(8,128)S(1)} %copy-done.4, bf16[4096,512]{1,0:T(8,128)(2,1)} %bitcast.23), custom_call_target="tpu_custom_call" | custom-call | flops 1073741824 | bytes 6553600 | tf_op jit(solution)/shard_map/project/pallas_call | solution.py:58
  239.8 6.6 %project.14.q_ref = bf16[256,1024]{1,0:T(8,128)(2,1)S(1)} custom-call(s32[1]{0:T(128)} %constant.113.clone.1.offsets, bf16[256,4096]{1,0:T(8,128)(2,1)} %collective-permute-done.8.x_ref, f32[256,128]{1,0:T(8,128)S(1)} %pad_maximum_fusion.4.cos_ref, f32[256,128]{1,0:T(8,128)S(1)} %copy-done.4, bf16[4096,1024]{1,0:T(8,128)(2,1)} %refs_0_.3), custom_call_target="tpu_custom_call" | custom-call | flops 2147483648 | bytes 11010048 | tf_op jit(solution)/shard_map/project/pallas_call | solution.py:58
  246.4 13.4 %collective-permute-done.18.refs_2_.refs_3_ = bf16[512,512]{1,0:T(8,128)(2,1)S(1)} collective-permute-done((bf16[512,512]{1,0:T(8,128)(2,1)S(1)}, bf16[512,512]{1,0:T(8,128)(2,1)S(1)}, u32[]{:S(2)}, u32[]{:S(2)}) %collective-permute-start.18) | collective-permute-done | bytes 524320 | tf_op jit(solution)/shard_map/ppermute | solution.py:426
  262.9 14.6 %attend.6.refs_0_ = bf16[256,1024]{1,0:T(8,128)(2,1)S(1)} custom-call(s32[16]{0:T(128)S(1)} %fusion.12.page_rows, s32[4]{0:T(128)S(1)} %add_bitcast_fusion.1.bounds, bf16[256,1024]{1,0:T(8,128)(2,1)S(1)} %project.14.q_ref, s32[256,128]{1,0:T(8,128)S(1)} %get-tuple-element.36.row_ref, bf16[2048,1024]{1,0:T(8,128)(2,1)} %constant_dynamic-update-slice_fusion.2.pk_ref.pv_ref, ...), custom_call_target="tpu_custom_call" | custom-call | flops 5368709120 | bytes 4718592 | tf_op jit(solution)/shard_map/attend/pallas_call | solution.py:197
  277.5 6.8 %project.15.q_ref = bf16[256,1024]{1,0:T(8,128)(2,1)S(1)} custom-call(s32[8]{0:T(128)S(1)} %fusion.13.offsets, bf16[256,4096]{1,0:T(8,128)(2,1)} %collective-permute-done.8.x_ref, f32[256,128]{1,0:T(8,128)S(1)} %pad_maximum_fusion.4.cos_ref, f32[256,128]{1,0:T(8,128)S(1)} %copy-done.4, bf16[512,1024]{1,0:T(8,128)(2,1)} %collective-permute-done.19.refs_0_, ...), custom_call_target="tpu_custom_call" | custom-call | flops 2147483648 | bytes 11010048 | tf_op jit(solution)/shard_map/project/pallas_call | solution.py:58
  284.3 3.8 collective-permute-done.28.refs_2_.refs_3_
  288.0 14.6 %attend.7.refs_1_ = bf16[256,1024]{1,0:T(8,128)(2,1)S(1)} custom-call(s32[16]{0:T(128)S(1)} %fusion.12.page_rows, s32[4]{0:T(128)S(1)} %add_bitcast_fusion.1.bounds, bf16[256,1024]{1,0:T(8,128)(2,1)S(1)} %project.15.q_ref, s32[256,128]{1,0:T(8,128)S(1)} %get-tuple-element.36.row_ref, bf16[2048,1024]{1,0:T(8,128)(2,1)} %constant_dynamic-update-slice_fusion.2.pk_ref.pv_ref, ...), custom_call_target="tpu_custom_call" | custom-call | flops 5368709120 | bytes 4718592 | tf_op jit(solution)/shard_map/attend/pallas_call | solution.py:197
  304.0 11.3 %outward.3 = bf16[256,4096]{1,0:T(8,128)(2,1)} custom-call(s32[8]{0:T(128)S(1)} %fusion.14.offsets, bf16[256,1024]{1,0:T(8,128)(2,1)S(1)} %attend.6.refs_0_, bf16[256,1024]{1,0:T(8,128)(2,1)S(1)} %attend.7.refs_1_, bf16[1024,4096]{1,0:T(8,128)(2,1)} %refs_2_.3, bf16[128,4096]{1,0:T(8,128)(2,1)S(1)} %collective-permute-done.29.refs_3_, ...), custom_call_target="tpu_custom_call" | custom-call | flops 4294967296 | bytes 18874368 | tf_op jit(solution)/shard_map/outward/pallas_call | solution.py:252
  315.3 8.5 %collective-permute-start.37 = (bf16[256,4096]{1,0:T(8,128)(2,1)}, bf16[256,4096]{1,0:T(8,128)(2,1)S(1)}, u32[]{:S(2)}, u32[]{:S(2)}) collective-permute-start(bf16[256,4096]{1,0:T(8,128)(2,1)} %outward.3), channel_id=1, source_target_pairs={{0,1},{1,0},{2,3},{3,2},{4,5},{5,4},{6,7},{7,6},{8,9},{9,8},{10,11... | collective-permute-start | bytes 6291464 | tf_op jit(solution)/shard_map/ppermute | solution.py:405
  327.1 6.1 %project.8.q_ref = bf16[256,1024]{1,0:T(8,128)(2,1)S(1)} custom-call(s32[1]{0:T(128)} %constant.113.clone.1.offsets, bf16[256,4096]{1,0:T(8,128)(2,1)S(1)} %copy-done.1, f32[256,128]{1,0:T(8,128)S(1)} %pad_maximum_fusion.2.cos_ref, f32[256,128]{1,0:T(8,128)S(1)} %pad_maximum_fusion.3.sin_ref, bf16[4096,1024]{1,0:T(8,128)(2,1)} %refs_0_.3), custom_call_target="tpu_custom_call" | custom-call | flops 2147483648 | bytes 11010048 | tf_op jit(solution)/shard_map/project/pallas_call | solution.py:58
  333.3 20.0 %attend.4.refs_0_ = bf16[256,1024]{1,0:T(8,128)(2,1)S(1)} custom-call(s32[16]{0:T(128)S(1)} %fusion.12.page_rows, s32[4]{0:T(128)S(1)} %add_bitcast_fusion.bounds, bf16[256,1024]{1,0:T(8,128)(2,1)S(1)} %project.8.q_ref, s32[256,128]{1,0:T(8,128)S(1)} %get-tuple-element.35.row_ref, bf16[2048,1024]{1,0:T(8,128)(2,1)} %constant_dynamic-update-slice_fusion.2.pk_ref.pv_ref, ...), custom_call_target="tpu_custom_call" | custom-call | flops 5368709120 | bytes 4718592 | tf_op jit(solution)/shard_map/attend/pallas_call | solution.py:197
  353.3 6.8 %project.13.q_ref = bf16[256,1024]{1,0:T(8,128)(2,1)S(1)} custom-call(s32[8]{0:T(128)S(1)} %fusion.13.offsets, bf16[256,4096]{1,0:T(8,128)(2,1)} %copy-done, f32[256,128]{1,0:T(8,128)S(1)} %pad_maximum_fusion.2.cos_ref, f32[256,128]{1,0:T(8,128)S(1)} %pad_maximum_fusion.3.sin_ref, bf16[512,1024]{1,0:T(8,128)(2,1)} %collective-permute-done.19.refs_0_, ...), custom_call_target="tpu_custom_call" | custom-call | flops 2147483648 | bytes 11010048 | tf_op jit(solution)/shard_map/project/pallas_call | solution.py:58
  360.1 19.8 %attend.5.refs_1_ = bf16[256,1024]{1,0:T(8,128)(2,1)S(1)} custom-call(s32[16]{0:T(128)S(1)} %fusion.12.page_rows, s32[4]{0:T(128)S(1)} %add_bitcast_fusion.bounds, bf16[256,1024]{1,0:T(8,128)(2,1)S(1)} %project.13.q_ref, s32[256,128]{1,0:T(8,128)S(1)} %get-tuple-element.35.row_ref, bf16[2048,1024]{1,0:T(8,128)(2,1)} %constant_dynamic-update-slice_fusion.2.pk_ref.pv_ref, ...), custom_call_target="tpu_custom_call" | custom-call | flops 5368709120 | bytes 4718592 | tf_op jit(solution)/shard_map/attend/pallas_call | solution.py:197
  379.8 11.3 %outward.2 = bf16[256,4096]{1,0:T(8,128)(2,1)} custom-call(s32[8]{0:T(128)S(1)} %fusion.14.offsets, bf16[256,1024]{1,0:T(8,128)(2,1)S(1)} %attend.4.refs_0_, bf16[256,1024]{1,0:T(8,128)(2,1)S(1)} %attend.5.refs_1_, bf16[1024,4096]{1,0:T(8,128)(2,1)} %refs_2_.3, bf16[128,4096]{1,0:T(8,128)(2,1)S(1)} %collective-permute-done.29.refs_3_, ...), custom_call_target="tpu_custom_call" | custom-call | flops 4294967296 | bytes 18874368 | tf_op jit(solution)/shard_map/outward/pallas_call | solution.py:252
  391.2 3.7 add_convert_fusion
  (155 shorter events, 66.1 us)
Async XLA Ops:
  1.0 27.0 %collective-permute-start = (bf16[256,512]{1,0:T(8,128)(2,1)S(1)}, bf16[256,512]{1,0:T(8,128)(2,1)S(1)}, u32[]{:S(2)}, u32[]{:S(2)}) collective-permute-start(bf16[256,512]{1,0:T(8,128)(2,1)S(1)} %bitcast.26), channel_id=1, source_target_pairs={{0,2},{1,3},{2,0},{3,1},{4,6},{5,7},{6,4},{7,5},{8,10},{9,11},{10,... | collective-permute-start | bytes 786440 | tf_op jit(solution)/shard_map/ppermute | solution.py:405
  5.3 32.9 %collective-permute-start.10 = (bf16[512,512]{1,0:T(8,128)(2,1)S(1)}, bf16[512,512]{1,0:T(8,128)(2,1)}, u32[]{:S(2)}, u32[]{:S(2)}) collective-permute-start(bf16[512,512]{1,0:T(8,128)(2,1)S(1)} %bitcast.28), channel_id=1, source_target_pairs={{0,2},{1,3},{2,0},{3,1},{4,6},{5,7},{6,4},{7,5},{8,10},{9,11},{10,... | collective-permute-start | bytes 1572872 | tf_op jit(solution)/shard_map/ppermute | solution.py:405
  30.7 25.4 %collective-permute-start.4 = (bf16[256,1024]{1,0:T(8,128)(2,1)}, bf16[256,1024]{1,0:T(8,128)(2,1)}, u32[]{:S(2)}, u32[]{:S(2)}) collective-permute-start(bf16[256,1024]{1,0:T(8,128)(2,1)} %get-tuple-element.17), channel_id=1, source_target_pairs={{0,16},{4,20},{8,24},{12,28},{16,0},{20,4},{24,8},{28,12},{1,17},{... | collective-permute-start | bytes 1572872 | tf_op jit(solution)/shard_map/ppermute | solution.py:408
  30.9 25.3 %collective-permute-start.2 = (bf16[256,1024]{1,0:T(8,128)(2,1)}, bf16[256,1024]{1,0:T(8,128)(2,1)}, u32[]{:S(2)}, u32[]{:S(2)}) collective-permute-start(bf16[256,1024]{1,0:T(8,128)(2,1)} %get-tuple-element.17), channel_id=1, source_target_pairs={{0,8},{4,12},{8,0},{12,4},{16,24},{20,28},{24,16},{28,20},{1,9},{5... | collective-permute-start | bytes 1572872 | tf_op jit(solution)/shard_map/ppermute | solution.py:408
  32.7 24.7 %collective-permute-start.1 = (bf16[256,1024]{1,0:T(8,128)(2,1)}, bf16[256,1024]{1,0:T(8,128)(2,1)}, u32[]{:S(2)}, u32[]{:S(2)}) collective-permute-start(bf16[256,1024]{1,0:T(8,128)(2,1)} %get-tuple-element.17), channel_id=1, source_target_pairs={{0,4},{4,0},{8,12},{12,8},{16,20},{20,16},{24,28},{28,24},{1,5},{5... | collective-permute-start | bytes 1572872 | tf_op jit(solution)/shard_map/ppermute | solution.py:408
  38.2 29.2 %collective-permute-start.16 = (bf16[512,512]{1,0:T(8,128)(2,1)}, bf16[512,512]{1,0:T(8,128)(2,1)}, u32[]{:S(2)}, u32[]{:S(2)}) collective-permute-start(bf16[512,512]{1,0:T(8,128)(2,1)} %collective-permute-done.10.refs_0_), channel_id=1, source_target_pairs={{0,24},{4,28},{8,16},{12,20},{16,8},{20,12},{24,0},{28,4},{1,25},{... | collective-permute-start | bytes 1572872 | tf_op jit(solution)/shard_map/ppermute | solution.py:408
  44.9 69.2 %collective-permute-start.29 = (bf16[128,4096]{1,0:T(8,128)(2,1)}, bf16[128,4096]{1,0:T(8,128)(2,1)S(1)}, u32[]{:S(2)}, u32[]{:S(2)}) collective-permute-start(bf16[128,4096]{1,0:T(8,128)(2,1)} %constant_dynamic-slice_fusion), channel_id=1, source_target_pairs={{0,2},{1,3},{2,0},{3,1},{4,6},{5,7},{6,4},{7,5},{8,10},{9,11},{10,... | collective-permute-start | bytes 3145736 | tf_op jit(solution)/shard_map/ppermute | solution.py:405
  56.1 78.4 %collective-permute-start.19 = (bf16[512,1024]{1,0:T(8,128)(2,1)}, bf16[512,1024]{1,0:T(8,128)(2,1)}, u32[]{:S(2)}, u32[]{:S(2)}) collective-permute-start(bf16[512,1024]{1,0:T(8,128)(2,1)} %constant_dynamic-slice_fusion.1), channel_id=1, source_target_pairs={{0,2},{1,3},{2,0},{3,1},{4,6},{5,7},{6,4},{7,5},{8,10},{9,11},{10,... | collective-permute-start | bytes 3145736 | tf_op jit(solution)/shard_map/ppermute | solution.py:405
  56.2 19.3 %collective-permute-start.14 = (bf16[512,512]{1,0:T(8,128)(2,1)}, bf16[512,512]{1,0:T(8,128)(2,1)}, u32[]{:S(2)}, u32[]{:S(2)}) collective-permute-start(bf16[512,512]{1,0:T(8,128)(2,1)} %collective-permute-done.10.refs_0_), channel_id=1, source_target_pairs={{0,16},{4,20},{8,24},{12,28},{16,0},{20,4},{24,8},{28,12},{1,17},{... | collective-permute-start | bytes 1572872 | tf_op jit(solution)/shard_map/ppermute | solution.py:408
  57.5 19.7 %collective-permute-start.12 = (bf16[512,512]{1,0:T(8,128)(2,1)}, bf16[512,512]{1,0:T(8,128)(2,1)}, u32[]{:S(2)}, u32[]{:S(2)}) collective-permute-start(bf16[512,512]{1,0:T(8,128)(2,1)} %collective-permute-done.10.refs_0_), channel_id=1, source_target_pairs={{0,8},{4,12},{8,0},{12,4},{16,24},{20,28},{24,16},{28,20},{1,9},{5... | collective-permute-start | bytes 1572872 | tf_op jit(solution)/shard_map/ppermute | solution.py:408
  75.5 136.8 %collective-permute-start.8 = (bf16[256,4096]{1,0:T(8,128)(2,1)S(1)}, bf16[256,4096]{1,0:T(8,128)(2,1)}, u32[]{:S(2)}, u32[]{:S(2)}) collective-permute-start(bf16[256,4096]{1,0:T(8,128)(2,1)S(1)} %fusion.2.x_ref), channel_id=1, source_target_pairs={{0,1},{1,0},{2,3},{3,2},{4,5},{5,4},{6,7},{7,6},{8,9},{9,8},{10,11... | collective-permute-start | bytes 6291464 | tf_op jit(solution)/shard_map/ppermute | solution.py:405
  77.2 58.7 %collective-permute-start.7 = (bf16[256,1024]{1,0:T(8,128)(2,1)}, bf16[256,1024]{1,0:T(8,128)(2,1)S(1)}, u32[]{:S(2)}, u32[]{:S(2)}) collective-permute-start(bf16[256,1024]{1,0:T(8,128)(2,1)} %collective-permute-done.6), channel_id=1, source_target_pairs={{0,4},{4,0},{8,12},{12,8},{16,20},{20,16},{24,28},{28,24},{1,5},{5... | collective-permute-start | bytes 1572872 | tf_op jit(solution)/shard_map/ppermute | solution.py:408
  77.2 60.2 %collective-permute-start.5 = (bf16[256,1024]{1,0:T(8,128)(2,1)}, bf16[256,1024]{1,0:T(8,128)(2,1)S(1)}, u32[]{:S(2)}, u32[]{:S(2)}) collective-permute-start(bf16[256,1024]{1,0:T(8,128)(2,1)} %collective-permute-done.4), channel_id=1, source_target_pairs={{0,4},{4,0},{8,12},{12,8},{16,20},{20,16},{24,28},{28,24},{1,5},{5... | collective-permute-start | bytes 1572872 | tf_op jit(solution)/shard_map/ppermute | solution.py:408
  114.1 32.1 %collective-permute-start.3 = (bf16[256,1024]{1,0:T(8,128)(2,1)}, bf16[256,1024]{1,0:T(8,128)(2,1)}, u32[]{:S(2)}, u32[]{:S(2)}) collective-permute-start(bf16[256,1024]{1,0:T(8,128)(2,1)} %collective-permute-done.2), channel_id=1, source_target_pairs={{0,4},{4,0},{8,12},{12,8},{16,20},{20,16},{24,28},{28,24},{1,5},{5... | collective-permute-start | bytes 1572872 | tf_op jit(solution)/shard_map/ppermute | solution.py:408
  134.5 27.1 %collective-permute-start.35 = (bf16[128,4096]{1,0:T(8,128)(2,1)S(1)}, bf16[128,4096]{1,0:T(8,128)(2,1)}, u32[]{:S(2)}, u32[]{:S(2)}) collective-permute-start(bf16[128,4096]{1,0:T(8,128)(2,1)S(1)} %collective-permute-done.29.refs_3_), channel_id=1, source_target_pairs={{0,24},{4,28},{8,16},{12,20},{16,8},{20,12},{24,0},{28,4},{1,25},{... | collective-permute-start | bytes 3145736 | tf_op jit(solution)/shard_map/ppermute | solution.py:408
  135.9 48.2 %collective-permute-start.33 = (bf16[128,4096]{1,0:T(8,128)(2,1)S(1)}, bf16[128,4096]{1,0:T(8,128)(2,1)}, u32[]{:S(2)}, u32[]{:S(2)}) collective-permute-start(bf16[128,4096]{1,0:T(8,128)(2,1)S(1)} %collective-permute-done.29.refs_3_), channel_id=1, source_target_pairs={{0,16},{4,20},{8,24},{12,28},{16,0},{20,4},{24,8},{28,12},{1,17},{... | collective-permute-start | bytes 3145736 | tf_op jit(solution)/shard_map/ppermute | solution.py:408
  149.6 67.2 %collective-permute-start.31 = (bf16[128,4096]{1,0:T(8,128)(2,1)S(1)}, bf16[128,4096]{1,0:T(8,128)(2,1)S(1)}, u32[]{:S(2)}, u32[]{:S(2)}) collective-permute-start(bf16[128,4096]{1,0:T(8,128)(2,1)S(1)} %collective-permute-done.29.refs_3_), channel_id=1, source_target_pairs={{0,8},{4,12},{8,0},{12,4},{16,24},{20,28},{24,16},{28,20},{1,9},{5... | collective-permute-start | bytes 3145736 | tf_op jit(solution)/shard_map/ppermute | solution.py:408
  153.5 67.7 %collective-permute-start.25 = (bf16[512,1024]{1,0:T(8,128)(2,1)}, bf16[512,1024]{1,0:T(8,128)(2,1)S(1)}, u32[]{:S(2)}, u32[]{:S(2)}) collective-permute-start(bf16[512,1024]{1,0:T(8,128)(2,1)} %collective-permute-done.19.refs_0_), channel_id=1, source_target_pairs={{0,24},{4,28},{8,16},{12,20},{16,8},{20,12},{24,0},{28,4},{1,25},{... | collective-permute-start | bytes 3145736 | tf_op jit(solution)/shard_map/ppermute | solution.py:408
  161.6 64.1 %collective-permute-start.23 = (bf16[512,1024]{1,0:T(8,128)(2,1)}, bf16[512,1024]{1,0:T(8,128)(2,1)S(1)}, u32[]{:S(2)}, u32[]{:S(2)}) collective-permute-start(bf16[512,1024]{1,0:T(8,128)(2,1)} %collective-permute-done.19.refs_0_), channel_id=1, source_target_pairs={{0,16},{4,20},{8,24},{12,28},{16,0},{20,4},{24,8},{28,12},{1,17},{... | collective-permute-start | bytes 3145736 | tf_op jit(solution)/shard_map/ppermute | solution.py:408
  184.1 43.7 %collective-permute-start.21 = (bf16[512,1024]{1,0:T(8,128)(2,1)}, bf16[512,1024]{1,0:T(8,128)(2,1)S(1)}, u32[]{:S(2)}, u32[]{:S(2)}) collective-permute-start(bf16[512,1024]{1,0:T(8,128)(2,1)} %collective-permute-done.19.refs_0_), channel_id=1, source_target_pairs={{0,8},{4,12},{8,0},{12,4},{16,24},{20,28},{24,16},{28,20},{1,9},{5... | collective-permute-start | bytes 3145736 | tf_op jit(solution)/shard_map/ppermute | solution.py:408
  212.3 19.9 %collective-permute-start.20 = (bf16[512,1024]{1,0:T(8,128)(2,1)}, bf16[512,1024]{1,0:T(8,128)(2,1)S(1)}, u32[]{:S(2)}, u32[]{:S(2)}) collective-permute-start(bf16[512,1024]{1,0:T(8,128)(2,1)} %collective-permute-done.19.refs_0_), channel_id=1, source_target_pairs={{0,4},{4,0},{8,12},{12,8},{16,20},{20,16},{24,28},{28,24},{1,5},{5... | collective-permute-start | bytes 3145736 | tf_op jit(solution)/shard_map/ppermute | solution.py:408
  221.2 40.7 %collective-permute-start.26 = (bf16[512,1024]{1,0:T(8,128)(2,1)S(1)}, bf16[512,1024]{1,0:T(8,128)(2,1)}, u32[]{:S(2)}, u32[]{:S(2)}) collective-permute-start(bf16[512,1024]{1,0:T(8,128)(2,1)S(1)} %collective-permute-done.25.refs_6_), channel_id=1, source_target_pairs={{0,4},{4,0},{8,12},{12,8},{16,20},{20,16},{24,28},{28,24},{1,5},{5... | collective-permute-start | bytes 3145736 | tf_op jit(solution)/shard_map/ppermute | solution.py:408
  225.7 36.7 %collective-permute-start.24 = (bf16[512,1024]{1,0:T(8,128)(2,1)S(1)}, bf16[512,1024]{1,0:T(8,128)(2,1)}, u32[]{:S(2)}, u32[]{:S(2)}) collective-permute-start(bf16[512,1024]{1,0:T(8,128)(2,1)S(1)} %collective-permute-done.23.refs_4_), channel_id=1, source_target_pairs={{0,4},{4,0},{8,12},{12,8},{16,20},{20,16},{24,28},{28,24},{1,5},{5... | collective-permute-start | bytes 3145736 | tf_op jit(solution)/shard_map/ppermute | solution.py:408
  227.8 34.7 %collective-permute-start.22 = (bf16[512,1024]{1,0:T(8,128)(2,1)S(1)}, bf16[512,1024]{1,0:T(8,128)(2,1)S(1)}, u32[]{:S(2)}, u32[]{:S(2)}) collective-permute-start(bf16[512,1024]{1,0:T(8,128)(2,1)S(1)} %collective-permute-done.21.refs_2_), channel_id=1, source_target_pairs={{0,4},{4,0},{8,12},{12,8},{16,20},{20,16},{24,28},{28,24},{1,5},{5... | collective-permute-start | bytes 3145736 | tf_op jit(solution)/shard_map/ppermute | solution.py:408
  232.2 27.6 %collective-permute-start.18 = (bf16[512,512]{1,0:T(8,128)(2,1)S(1)}, bf16[512,512]{1,0:T(8,128)(2,1)S(1)}, u32[]{:S(2)}, u32[]{:S(2)}) collective-permute-start(bf16[512,512]{1,0:T(8,128)(2,1)S(1)} %pad_maximum_fusion.1.refs_4_.refs_5_), channel_id=1, source_target_pairs={{0,2},{1,3},{2,4},{3,5},{4,6},{5,7},{6,8},{7,9},{8,10},{9,11},{10,... | collective-permute-start | bytes 1572872 | tf_op jit(solution)/shard_map/ppermute | solution.py:426
  234.1 25.6 %collective-permute-start.9 = (bf16[512,512]{1,0:T(8,128)(2,1)S(1)}, bf16[512,512]{1,0:T(8,128)(2,1)S(1)}, u32[]{:S(2)}, u32[]{:S(2)}) collective-permute-start(bf16[512,512]{1,0:T(8,128)(2,1)S(1)} %pad_maximum_fusion.refs_4_.refs_5_), channel_id=1, source_target_pairs={{0,4},{1,5},{2,6},{3,7},{4,8},{5,9},{6,10},{7,11},{8,12},{9,13},{1... | collective-permute-start | bytes 1572872 | tf_op jit(solution)/shard_map/ppermute | solution.py:426
  259.7 42.9 %collective-permute-start.30 = (bf16[128,4096]{1,0:T(8,128)(2,1)S(1)}, bf16[128,4096]{1,0:T(8,128)(2,1)S(1)}, u32[]{:S(2)}, u32[]{:S(2)}) collective-permute-start(bf16[128,4096]{1,0:T(8,128)(2,1)S(1)} %collective-permute-done.29.refs_3_), channel_id=1, source_target_pairs={{0,4},{4,0},{8,12},{12,8},{16,20},{20,16},{24,28},{28,24},{1,5},{5... | collective-permute-start | bytes 3145736 | tf_op jit(solution)/shard_map/ppermute | solution.py:408
  259.7 28.3 %collective-permute-start.28 = (bf16[512,512]{1,0:T(8,128)(2,1)S(1)}, bf16[512,512]{1,0:T(8,128)(2,1)S(1)}, u32[]{:S(2)}, u32[]{:S(2)}) collective-permute-start(bf16[512,512]{1,0:T(8,128)(2,1)S(1)} %pad_maximum_fusion.refs_4_.refs_5_), channel_id=1, source_target_pairs={{0,2},{1,3},{2,4},{3,5},{4,6},{5,7},{6,8},{7,9},{8,10},{9,11},{10,... | collective-permute-start | bytes 1572872 | tf_op jit(solution)/shard_map/ppermute | solution.py:426
  261.9 40.8 %collective-permute-start.36 = (bf16[128,4096]{1,0:T(8,128)(2,1)}, bf16[128,4096]{1,0:T(8,128)(2,1)S(1)}, u32[]{:S(2)}, u32[]{:S(2)}) collective-permute-start(bf16[128,4096]{1,0:T(8,128)(2,1)} %collective-permute-done.35.refs_9_), channel_id=1, source_target_pairs={{0,4},{4,0},{8,12},{12,8},{16,20},{20,16},{24,28},{28,24},{1,5},{5... | collective-permute-start | bytes 3145736 | tf_op jit(solution)/shard_map/ppermute | solution.py:408
  262.4 40.3 %collective-permute-start.34 = (bf16[128,4096]{1,0:T(8,128)(2,1)}, bf16[128,4096]{1,0:T(8,128)(2,1)S(1)}, u32[]{:S(2)}, u32[]{:S(2)}) collective-permute-start(bf16[128,4096]{1,0:T(8,128)(2,1)} %collective-permute-done.33.refs_7_), channel_id=1, source_target_pairs={{0,4},{4,0},{8,12},{12,8},{16,20},{20,16},{24,28},{28,24},{1,5},{5... | collective-permute-start | bytes 3145736 | tf_op jit(solution)/shard_map/ppermute | solution.py:408
  262.5 40.2 %collective-permute-start.32 = (bf16[128,4096]{1,0:T(8,128)(2,1)S(1)}, bf16[128,4096]{1,0:T(8,128)(2,1)S(1)}, u32[]{:S(2)}, u32[]{:S(2)}) collective-permute-start(bf16[128,4096]{1,0:T(8,128)(2,1)S(1)} %collective-permute-done.31.refs_5_), channel_id=1, source_target_pairs={{0,4},{4,0},{8,12},{12,8},{16,20},{20,16},{24,28},{28,24},{1,5},{5... | collective-permute-start | bytes 3145736 | tf_op jit(solution)/shard_map/ppermute | solution.py:408
  315.3 75.8 %collective-permute-start.37 = (bf16[256,4096]{1,0:T(8,128)(2,1)}, bf16[256,4096]{1,0:T(8,128)(2,1)S(1)}, u32[]{:S(2)}, u32[]{:S(2)}) collective-permute-start(bf16[256,4096]{1,0:T(8,128)(2,1)} %outward.3), channel_id=1, source_target_pairs={{0,1},{1,0},{2,3},{3,2},{4,5},{5,4},{6,7},{7,6},{8,9},{9,8},{10,11... | collective-permute-start | bytes 6291464 | tf_op jit(solution)/shard_map/ppermute | solution.py:405
  (29 other events, 441.6 us)
